TPU v7x, 32 devices: a whole 2x2x4 slice. The times are simulated.
32 devices in a mesh: dp: 4 (over y, x), ctx: 8 (over z, core).
Axes of the slice: x: 2, y: 2, z: 4, core: 2. Of those that a mesh axis runs over, the one named last changes fastest.
Arguments:
- hidden_in: bfloat16 [4, 16, 128, 1024], P('dp', 'ctx'), may hold values from -6 to 6
- cotangent: bfloat16 [4, 16, 128, 1024], P('dp', 'ctx'), may hold values from -6 to 6
- lengths: int32 [4], P('dp'), may hold values from 512 to 2048, as said below
- block_map: int32 [16], replicated, may hold values from 0 to 15, as said below
- norm_in: float32 [1024], replicated, may hold values from 0.1 to 1.9
- q_weight: bfloat16 [1024, 1024], P('dp'), may hold values from -0.1875 to 0.1875
- kv_weight: bfloat16 [1024, 1024], P('dp'), may hold values from -0.1875 to 0.1875
- q_gain: float32 [64], replicated, may hold values from 0.1 to 1.9
- k_gain: float32 [64], replicated, may hold values from 0.1 to 1.9
- out_weight: bfloat16 [1024, 1024], P('dp'), may hold values from -6 to 6
- norm_mid: float32 [1024], replicated, may hold values from 0.1 to 1.9
- gate_weight: bfloat16 [1024, 4608], P('dp'), may hold values from -0.1875 to 0.1875
- up_weight: bfloat16 [1024, 4608], P('dp'), may hold values from -0.1875 to 0.1875
- down_weight: bfloat16 [4608, 1024], P('dp'), may hold values from -0.09375 to 0.09375
Outputs:
- output: bfloat16 [4, 16, 128, 1024], P('dp', 'ctx')
- input_grad: float32 [4, 16, 128, 1024], P('dp', 'ctx')
- norm_in_grad: float32 [1024], P('ctx')
- q_weight_grad: float32 [1024, 1024], P('ctx')
- kv_weight_grad: float32 [1024, 1024], P('ctx')
- q_gain_grad: float32 [64], P('ctx')
- k_gain_grad: float32 [64], P('ctx')
- out_weight_grad: float32 [1024, 1024], P('ctx')
- norm_mid_grad: float32 [1024], P('ctx')
- gate_weight_grad: float32 [1024, 4608], P('ctx')
- up_weight_grad: float32 [1024, 4608], P('ctx')
- down_weight_grad: float32 [4608, 1024], P('ctx')
Inputs may be any that keep to these rules, and one draw needn't show every extreme that they name: Of the 2 sequences held by dp indices 2 i and 2 i + 1 (the last index alone where their number is odd), one, which one varies, has length 2048; the other lengths vary. `block_map`: A permutation of the block numbers; slots 2 c and 2 c + 1 hold blocks b and 15 - b with b < 8.
All inputs are finite; a program needn't handle non-finite values.
Results may differ from a plain program's by a relative error of at most 0.02.
Values may be sent and summed in bfloat16 or wider, within the bound.
A program may use at most 256 MiB of HBM per device.

v0:
```python
import math

import jax
import jax.numpy as jnp
from jax import lax
from jax.sharding import PartitionSpec as P

epsilon = 1e-05
rope_base = 1000000.0
masked_score = -1e30


def dense_dot(left, right):
    return jnp.dot(left, right, preferred_element_type=jnp.float32)


def outer_dot(left, right):
    return lax.dot_general(
        left, right, (((0,), (0,)), ((), ())), preferred_element_type=jnp.float32
    )


def back_dot(grad_rows, weight_rows):
    return lax.dot_general(
        grad_rows, weight_rows, (((1,), (1,)), ((), ())), preferred_element_type=jnp.float32
    )


def root_scale(vector):
    return lax.rsqrt(jnp.mean(vector * vector, axis=-1, keepdims=True) + epsilon)


def norm_back(grad_rows, value_rows, scale_rows):
    cubed = scale_rows * scale_rows * scale_rows
    return scale_rows * grad_rows - value_rows * cubed * jnp.mean(
        grad_rows * value_rows, axis=-1, keepdims=True
    )


def tables(positions, head_size):
    half_size = head_size // 2
    inverse = rope_base ** (-2.0 * jnp.arange(half_size, dtype=jnp.float32) / head_size)
    angles = positions.astype(jnp.float32)[:, None] * inverse[None, :]
    return (jnp.cos(angles)[:, None, :], jnp.sin(angles)[:, None, :])


def rotate(vector, cosine, sine_table):
    half_size = vector.shape[-1] // 2
    first_half = vector[..., :half_size]
    second_half = vector[..., half_size:]
    return jnp.concatenate(
        [
            first_half * cosine - second_half * sine_table,
            second_half * cosine + first_half * sine_table,
        ],
        axis=-1,
    )


def unrotate(vector, cosine, sine_table):
    half_size = vector.shape[-1] // 2
    first_half = vector[..., :half_size]
    second_half = vector[..., half_size:]
    return jnp.concatenate(
        [
            first_half * cosine + second_half * sine_table,
            second_half * cosine - first_half * sine_table,
        ],
        axis=-1,
    )


def per_device(
    hidden_in,
    cotangent,
    lengths,
    block_map,
    norm_in,
    q_weight,
    kv_weight,
    q_gain,
    k_gain,
    out_weight,
    norm_mid,
    gate_weight,
    up_weight,
    down_weight,
):
    seqs_local, pair_count, block_size, width = hidden_in.shape
    row_count = pair_count * block_size
    token_count = seqs_local * row_count
    head_size = q_gain.shape[0]
    head_count = width // head_size
    kv_width = kv_weight.shape[1] // 2
    kv_count = kv_width // head_size
    group_size = head_count // kv_count
    ctx_count = lax.axis_size("ctx")
    key_count = 2 * ctx_count * block_size
    tile_size = math.gcd(256, key_count)
    tile_count = key_count // tile_size
    score_scale = 1.0 / math.sqrt(head_size)
    offsets = jnp.arange(block_size, dtype=jnp.int32)
    own_blocks = lax.dynamic_slice_in_dim(block_map, lax.axis_index("ctx") * 2, 2)
    query_pos = (own_blocks[:, None] * block_size + offsets[None, :]).reshape(row_count)
    key_pos = (block_map[:, None] * block_size + offsets[None, :]).reshape(key_count)
    token_pos = jnp.tile(query_pos, seqs_local)
    query_place = jnp.tile(query_pos, group_size)
    cosine, sine_table = tables(token_pos, head_size)
    full_q, full_kv, full_out, full_gate, full_up, full_down = (
        lax.all_gather(q_weight, "dp", axis=0, tiled=True),
        lax.all_gather(kv_weight, "dp", axis=0, tiled=True),
        lax.all_gather(out_weight, "dp", axis=0, tiled=True),
        lax.all_gather(gate_weight, "dp", axis=0, tiled=True),
        lax.all_gather(up_weight, "dp", axis=0, tiled=True),
        lax.all_gather(down_weight, "dp", axis=0, tiled=True),
    )
    inputs = hidden_in.astype(jnp.float32).reshape(token_count, width)
    scale_in = root_scale(inputs)
    normed = (inputs * scale_in * norm_in).astype(jnp.bfloat16)
    q_raw = dense_dot(normed, full_q).reshape(token_count, head_count, head_size)
    kv_raw = dense_dot(normed, full_kv)
    k_raw = kv_raw[:, :kv_width].reshape(token_count, kv_count, head_size)
    values = kv_raw[:, kv_width:].astype(jnp.bfloat16)
    q_scale = root_scale(q_raw)
    k_scale = root_scale(k_raw)
    q_rot = rotate(q_raw * q_scale * q_gain, cosine, sine_table).astype(jnp.bfloat16)
    k_rot = rotate(k_raw * k_scale * k_gain, cosine, sine_table).astype(jnp.bfloat16)
    local_kv = jnp.concatenate([k_rot.reshape(token_count, kv_width), values], axis=1).reshape(
        seqs_local, pair_count, block_size, 2 * kv_width
    )
    whole_kv = lax.all_gather(local_kv, "ctx", axis=1, tiled=True)
    key_all = whole_kv[..., :kv_width].reshape(seqs_local, key_count, kv_count, head_size)
    value_all = whole_kv[..., kv_width:].reshape(seqs_local, key_count, kv_count, head_size)
    queries = (
        q_rot.reshape(seqs_local, row_count, kv_count, group_size, head_size)
        .transpose(0, 2, 3, 1, 4)
        .reshape(seqs_local, kv_count, group_size * row_count, head_size)
    )
    tile_starts = jnp.arange(tile_count, dtype=jnp.int32) * tile_size

    def tile_of(tile_start):
        key_tile = lax.dynamic_slice_in_dim(key_all, tile_start, tile_size, 1)
        value_tile = lax.dynamic_slice_in_dim(value_all, tile_start, tile_size, 1)
        key_place = lax.dynamic_slice_in_dim(key_pos, tile_start, tile_size, 0)
        scores = (
            jnp.einsum("snqd,sknd->snqk", queries, key_tile, preferred_element_type=jnp.float32)
            * score_scale
        )
        allowed = (key_place[None, None, None, :] <= query_place[None, None, :, None]) & (
            key_place[None, None, None, :] < lengths[:, None, None, None]
        )
        return (key_tile, value_tile, scores, allowed)

    def stat_step(state_in, tile_start):
        row_max, row_total = state_in
        _, _, scores, allowed = tile_of(tile_start)
        masked = jnp.where(allowed, scores, masked_score)
        new_max = jnp.maximum(row_max, jnp.max(masked, axis=-1))
        exp_terms = jnp.where(allowed, jnp.exp(masked - new_max[..., None]), 0.0)
        row_total = row_total * jnp.exp(row_max - new_max) + jnp.sum(exp_terms, axis=-1)
        return ((new_max, row_total), None)

    stat_shape = (seqs_local, kv_count, group_size * row_count)
    start_state = (
        jnp.full(stat_shape, masked_score, jnp.float32),
        jnp.zeros(stat_shape, jnp.float32),
    )
    (row_max, row_total), _ = lax.scan(stat_step, start_state, tile_starts)
    log_total = row_max + jnp.log(row_total)

    def value_step(running, tile_start):
        _, value_tile, scores, allowed = tile_of(tile_start)
        weights_tile = jnp.where(allowed, jnp.exp(scores - log_total[..., None]), 0.0).astype(
            jnp.bfloat16
        )
        return (
            running
            + jnp.einsum(
                "snqk,sknd->snqd", weights_tile, value_tile, preferred_element_type=jnp.float32
            ),
            None,
        )

    attended, _ = lax.scan(value_step, jnp.zeros(queries.shape, jnp.float32), tile_starts)

    def to_tokens(array):
        return (
            array.reshape(seqs_local, kv_count, group_size, row_count, head_size)
            .transpose(0, 3, 1, 2, 4)
            .reshape(token_count, width)
        )

    mixed_heads = to_tokens(attended).astype(jnp.bfloat16)
    residual = inputs + dense_dot(mixed_heads, full_out)
    scale_mid = root_scale(residual)
    normed_mid = (residual * scale_mid * norm_mid).astype(jnp.bfloat16)
    gate_value = dense_dot(normed_mid, full_gate)
    up_value = dense_dot(normed_mid, full_up)
    sigmoid_gate = jax.nn.sigmoid(gate_value)
    silu_gate = gate_value * sigmoid_gate
    hidden = (silu_gate * up_value).astype(jnp.bfloat16)
    output = (residual + dense_dot(hidden, full_down)).astype(jnp.bfloat16).reshape(hidden_in.shape)
    full_q, full_kv, full_out, full_gate, full_up, full_down = (
        lax.all_gather(q_weight, "dp", axis=0, tiled=True),
        lax.all_gather(kv_weight, "dp", axis=0, tiled=True),
        lax.all_gather(out_weight, "dp", axis=0, tiled=True),
        lax.all_gather(gate_weight, "dp", axis=0, tiled=True),
        lax.all_gather(up_weight, "dp", axis=0, tiled=True),
        lax.all_gather(down_weight, "dp", axis=0, tiled=True),
    )
    valid_rows = (query_pos[None, :] < lengths[:, None]).astype(jnp.float32).reshape(token_count, 1)
    cot_rows = cotangent.astype(jnp.float32).reshape(token_count, width) * valid_rows
    d_ffn = cot_rows.astype(jnp.bfloat16)
    down_grad = outer_dot(hidden, d_ffn)
    d_hidden = back_dot(d_ffn, full_down)
    d_gate = (
        d_hidden * up_value * sigmoid_gate * (1.0 + gate_value * (1.0 - sigmoid_gate))
    ).astype(jnp.bfloat16)
    d_up = (d_hidden * silu_gate).astype(jnp.bfloat16)
    gate_grad = outer_dot(normed_mid, d_gate)
    up_grad = outer_dot(normed_mid, d_up)
    d_mid = back_dot(d_gate, full_gate) + back_dot(d_up, full_up)
    mid_gain_grad = jnp.sum(d_mid * residual * scale_mid, axis=0)
    d_resid = cot_rows + norm_back(d_mid * norm_mid, residual, scale_mid)
    d_attn = d_resid.astype(jnp.bfloat16)
    out_grad = outer_dot(mixed_heads, d_attn)
    d_mixed = back_dot(d_attn, full_out).astype(jnp.bfloat16)
    d_heads = (
        d_mixed.reshape(seqs_local, row_count, kv_count, group_size, head_size)
        .transpose(0, 2, 3, 1, 4)
        .reshape(queries.shape)
    )
    row_delta = jnp.sum(d_heads.astype(jnp.float32) * attended, axis=-1)

    def grad_step(state_in, tile_start):
        d_query, d_keys, d_values = state_in
        key_tile, value_tile, scores, allowed = tile_of(tile_start)
        weights_tile = jnp.where(allowed, jnp.exp(scores - log_total[..., None]), 0.0)
        d_weights = jnp.einsum(
            "snqd,sknd->snqk", d_heads, value_tile, preferred_element_type=jnp.float32
        )
        d_scores = (weights_tile * (d_weights - row_delta[..., None]) * score_scale).astype(
            jnp.bfloat16
        )
        d_query = d_query + jnp.einsum(
            "snqk,sknd->snqd", d_scores, key_tile, preferred_element_type=jnp.float32
        )
        key_part = jnp.einsum(
            "snqk,snqd->sknd", d_scores, queries, preferred_element_type=jnp.float32
        )
        value_part = jnp.einsum(
            "snqk,snqd->sknd",
            weights_tile.astype(jnp.bfloat16),
            d_heads,
            preferred_element_type=jnp.float32,
        )
        d_keys = lax.dynamic_update_slice_in_dim(d_keys, key_part, tile_start, 1)
        d_values = lax.dynamic_update_slice_in_dim(d_values, value_part, tile_start, 1)
        return ((d_query, d_keys, d_values), None)

    kv_shape = (seqs_local, key_count, kv_count, head_size)
    grad_state = (
        jnp.zeros(queries.shape, jnp.float32),
        jnp.zeros(kv_shape, jnp.float32),
        jnp.zeros(kv_shape, jnp.float32),
    )
    (d_query, d_keys, d_values), _ = lax.scan(grad_step, grad_state, tile_starts)
    block_shape = (seqs_local, 2 * ctx_count, block_size, kv_width)
    own_keys, own_values = (
        lax.psum_scatter(
            d_keys.reshape(block_shape).astype(jnp.bfloat16), "ctx", scatter_dimension=1, tiled=True
        ).astype(jnp.float32),
        lax.psum_scatter(
            d_values.reshape(block_shape).astype(jnp.bfloat16),
            "ctx",
            scatter_dimension=1,
            tiled=True,
        ).astype(jnp.float32),
    )
    d_krot = own_keys.reshape(token_count, kv_count, head_size)
    d_vraw = own_values.reshape(token_count, kv_width)
    d_qrot = to_tokens(d_query).reshape(token_count, head_count, head_size)
    d_qnorm = unrotate(d_qrot, cosine, sine_table)
    d_knorm = unrotate(d_krot, cosine, sine_table)
    q_gain_grad = jnp.sum(d_qnorm * q_raw * q_scale, axis=(0, 1))
    k_gain_grad = jnp.sum(d_knorm * k_raw * k_scale, axis=(0, 1))
    d_qraw = (
        norm_back(d_qnorm * q_gain, q_raw, q_scale).reshape(token_count, width).astype(jnp.bfloat16)
    )
    d_kraw = norm_back(d_knorm * k_gain, k_raw, k_scale).reshape(token_count, kv_width)
    d_kvraw = jnp.concatenate([d_kraw, d_vraw], axis=1).astype(jnp.bfloat16)
    q_grad = outer_dot(normed, d_qraw)
    kv_grad = outer_dot(normed, d_kvraw)
    d_normed = back_dot(d_qraw, full_q) + back_dot(d_kvraw, full_kv)
    in_gain_grad = jnp.sum(d_normed * inputs * scale_in, axis=0)
    input_grad = (d_resid + norm_back(d_normed * norm_in, inputs, scale_in)).reshape(
        hidden_in.shape
    )
    gain_list = (in_gain_grad, q_gain_grad, k_gain_grad, mid_gain_grad)
    packed = jnp.concatenate(
        [gain_term.reshape(ctx_count, -1) for gain_term in gain_list], axis=1
    ).reshape(-1)
    share_gains, share_q, share_kv, share_out, share_gate, share_up, share_down = (
        lax.psum_scatter(
            packed.astype(jnp.bfloat16), "ctx", scatter_dimension=0, tiled=True
        ).astype(jnp.float32),
        lax.psum_scatter(
            q_grad.astype(jnp.bfloat16), "ctx", scatter_dimension=0, tiled=True
        ).astype(jnp.float32),
        lax.psum_scatter(
            kv_grad.astype(jnp.bfloat16), "ctx", scatter_dimension=0, tiled=True
        ).astype(jnp.float32),
        lax.psum_scatter(
            out_grad.astype(jnp.bfloat16), "ctx", scatter_dimension=0, tiled=True
        ).astype(jnp.float32),
        lax.psum_scatter(
            gate_grad.astype(jnp.bfloat16), "ctx", scatter_dimension=0, tiled=True
        ).astype(jnp.float32),
        lax.psum_scatter(
            up_grad.astype(jnp.bfloat16), "ctx", scatter_dimension=0, tiled=True
        ).astype(jnp.float32),
        lax.psum_scatter(
            down_grad.astype(jnp.bfloat16), "ctx", scatter_dimension=0, tiled=True
        ).astype(jnp.float32),
    )
    total_gains, total_q, total_kv, total_out, total_gate, total_up, total_down = (
        lax.psum(share_gains.astype(jnp.bfloat16), "dp").astype(jnp.float32),
        lax.psum(share_q.astype(jnp.bfloat16), "dp").astype(jnp.float32),
        lax.psum(share_kv.astype(jnp.bfloat16), "dp").astype(jnp.float32),
        lax.psum(share_out.astype(jnp.bfloat16), "dp").astype(jnp.float32),
        lax.psum(share_gate.astype(jnp.bfloat16), "dp").astype(jnp.float32),
        lax.psum(share_up.astype(jnp.bfloat16), "dp").astype(jnp.float32),
        lax.psum(share_down.astype(jnp.bfloat16), "dp").astype(jnp.float32),
    )
    wide_piece = width // ctx_count
    head_piece = head_size // ctx_count
    in_gain_share = total_gains[:wide_piece]
    q_gain_share = total_gains[wide_piece : wide_piece + head_piece]
    k_gain_share = total_gains[wide_piece + head_piece : wide_piece + 2 * head_piece]
    mid_gain_share = total_gains[wide_piece + 2 * head_piece :]
    return (
        output,
        input_grad,
        in_gain_share,
        total_q,
        total_kv,
        q_gain_share,
        k_gain_share,
        total_out,
        mid_gain_share,
        total_gate,
        total_up,
        total_down,
    )


def solution(mesh):
    return jax.shard_map(
        per_device,
        mesh=mesh,
        in_specs=(
            P("dp", "ctx", None, None),
            P("dp", "ctx", None, None),
            P("dp"),
            P(),
            P(),
            P("dp", None),
            P("dp", None),
            P(),
            P(),
            P("dp", None),
            P(),
            P("dp", None),
            P("dp", None),
            P("dp", None),
        ),
        out_specs=(
            P("dp", "ctx", None, None),
            P("dp", "ctx", None, None),
            P("ctx"),
            P("ctx", None),
            P("ctx", None),
            P("ctx"),
            P("ctx"),
            P("ctx", None),
            P("ctx"),
            P("ctx", None),
            P("ctx", None),
            P("ctx", None),
        ),
        check_vma=False,
    )
```

profile of v0, /device:TPU:0, one launch (start us, length us, event | category | flops | bytes accessed | tf_op | source)
XLA Modules:
  0.0 1293.5 jit_solution(18290252016960646901)
XLA Ops:
  12.8 35.1 %all-gather.8.cloned.1.call-done = bf16[1024,1024]{1,0:T(8,128)(2,1)} async-done(((bf16[256,1024]{1,0:T(8,128)(2,1)}), bf16[1024,1024]{1,0:T(8,128)(2,1)}) %all-gather.8.cloned.1.call-update) | async-done | bytes 2097168 | tf_op jit(solution)/shard_map/all_gather | solution.py:111
  60.9 24.2 %all-gather.12.cloned.1.call-done = bf16[1024,1024]{1,0:T(8,128)(2,1)} async-done(((bf16[256,1024]{1,0:T(8,128)(2,1)}), bf16[1024,1024]{1,0:T(8,128)(2,1)}) %all-gather.12.cloned.1.call-update) | async-done | bytes 2097168 | tf_op jit(solution)/shard_map/all_gather | solution.py:110
  89.9 44.5 %all-gather.10.cloned.1.call-done = bf16[1,16,128,1024]{3,2,0,1:T(8,128)(2,1)} async-done(((bf16[1,2,128,1024]{3,2,0,1:T(8,128)(2,1)}), bf16[1,16,128,1024]{3,2,0,1:T(8,128)(2,1)}) %all-gather.10.cloned.1.call-update) | async-done | bytes 4194320 | tf_op jit(solution)/shard_map/all_gather | solution.py:131
  134.4 3.9 fusion.75
  144.4 92.7 %while.39 = (s32[]{:T(128)}, f32[1,8,512]{2,1,0:T(8,128)S(1)}, f32[1,8,512]{2,1,0:T(8,128)S(1)}, s32[8]{0:T(128)}, s32[2048]{0:T(1024)}, /*index=5*/s32[1]{0:T(1...) while((s32[]{:T(128)}, f32[1,8,512]{2,1,0:T(8,128)S(1)}, ...), condition=%wide.region_6.7_spmd.clone, body=%wide.region_3.6_spmd.clone.sunk | while | flops 142889216 | bytes 9794234 | solution.py:168
  152.7 3.2 select_reduce_fusion.2
  164.3 3.2 select_reduce_fusion.2
  175.9 3.2 select_reduce_fusion.2
  187.5 3.2 select_reduce_fusion.2
  210.7 3.2 select_reduce_fusion.2
  222.3 3.2 select_reduce_fusion.2
  233.8 3.2 select_reduce_fusion.2
  237.1 4.5 copy.139
  241.6 4.1 reshape.674
  246.3 73.2 %while.40 = (s32[]{:T(128)}, f32[1,8,512,64]{2,3,1,0:T(8,128)}, s32[8]{0:T(128)}, s32[2048]{0:T(1024)}, s32[1]{0:T(128)}, /*index=5*/bf16[1,2048,8,64]{1,3,2,0:T...) while((s32[]{:T(128)}, f32[1,8,512,64]{2,3,1,0:T(8,128)}, ...), condition=%wide.region_8.9_spmd.clone, body=%wide.region_7.8_spmd.clone.sunk | while | flops 273416448 | bytes 3438780 | solution.py:184
  251.7 3.4 fusion.140
  260.5 3.8 fusion.140
  269.7 3.8 fusion.140
  278.9 4.0 fusion.140
  288.3 3.8 fusion.140
  297.4 3.8 fusion.140
  306.6 3.8 fusion.140
  315.8 3.7 fusion.140
  329.3 7.9 fusion.79
  337.2 29.1 %all-gather.18.cloned.1.call-done = bf16[1024,4608]{1,0:T(8,128)(2,1)} async-done(((bf16[256,4608]{1,0:T(8,128)(2,1)}), bf16[1024,4608]{1,0:T(8,128)(2,1)}) %all-gather.18.cloned.1.call-update) | async-done | bytes 9437200 | tf_op jit(solution)/shard_map/all_gather | solution.py:114
  366.4 8.0 fusion.80
  374.3 90.3 %all-gather.20.cloned.1.call-done = bf16[4608,1024]{1,0:T(8,128)(2,1)} async-done(((bf16[1152,1024]{1,0:T(8,128)(2,1)}), bf16[4608,1024]{1,0:T(8,128)(2,1)}) %all-gather.20.cloned.1.call-update) | async-done | bytes 9437200 | tf_op jit(solution)/shard_map/all_gather | solution.py:115
  464.6 10.1 multiply_convert_fusion
  474.7 6.9 fusion.81
  483.2 3.3 multiply_reduce_fusion
  499.1 176.8 %while.41 = (s32[]{:T(128)}, f32[1,8,512,64]{2,3,1,0:T(8,128)}, bf16[1,2048,8,64]{1,3,2,0:T(8,128)(2,1)}, bf16[1,2048,8,64]{1,3,2,0:T(8,128)(2,1)}, s32[8]{0:T(1...) while((s32[]{:T(128)}, f32[1,8,512,64]{2,3,1,0:T(8,128)}, ...), condition=%wide.region_13.14_spmd.clone, body=%wide.region_12.13_spmd.clone.sunk | while | flops 683409664 | bytes 78312312 | solution.py:267
  509.4 3.4 dynamic_update_slice.10
  517.6 3.5 dynamic_update_slice.11
  531.3 3.5 dynamic_update_slice.10
  540.0 3.5 dynamic_update_slice.11
  553.7 3.4 dynamic_update_slice.10
  562.3 3.4 dynamic_update_slice.11
  576.1 3.5 dynamic_update_slice.10
  584.7 3.4 dynamic_update_slice.11
  598.4 3.4 dynamic_update_slice.10
  607.0 3.4 dynamic_update_slice.11
  620.7 3.4 dynamic_update_slice.10
  629.2 3.5 dynamic_update_slice.11
  643.0 3.5 dynamic_update_slice.10
  651.6 3.4 dynamic_update_slice.11
  675.9 3.5 copy.163
  679.5 4.9 copy.144
  686.4 4.5 copy.150
  700.3 20.0 %reduce-scatter.9.cloned.1.call-done = bf16[1,2,128,512]{3,2,0,1:T(8,128)(2,1)} async-done(((bf16[1,16,128,512]{3,2,0,1:T(8,128)(2,1)}), bf16[1,2,128,512]{3,2,0,1:T(8,128)(2,1)}) %reduce-scatter.9.cloned.1.call-update) | async-done | bytes 262160 | tf_op jit(solution)/shard_map/reduce_scatter | solution.py:270
  729.6 27.4 %reduce-scatter.11.cloned.1.call-done = bf16[1,2,128,512]{3,2,1,0:T(8,128)(2,1)} async-done(((bf16[1,16,128,512]{3,2,1,0:T(8,128)(2,1)}), bf16[1,2,128,512]{3,2,1,0:T(8,128)(2,1)}) %reduce-scatter.11.cloned.1.call-update) | async-done | bytes 262160 | tf_op jit(solution)/shard_map/reduce_scatter | solution.py:273
  760.1 6.7 convolution_convert_fusion.2
  766.9 6.8 convolution_convert_fusion.1
  774.7 6.9 convolution_convert_fusion
  781.9 11.5 reduce-scatter.17.cloned.1.call-done
  793.4 36.7 %reduce-scatter.13.cloned.1.call-done = bf16[128,1024]{1,0:T(8,128)(2,1)} async-done(((bf16[1024,1024]{1,0:T(8,128)(2,1)}), bf16[128,1024]{1,0:T(8,128)(2,1)}) %reduce-scatter.13.cloned.1.call-update) | async-done | bytes 262160 | tf_op jit(solution)/shard_map/reduce_scatter | solution.py:307
  830.1 36.6 %reduce-scatter.15.cloned.1.call-done = bf16[128,1024]{1,0:T(8,128)(2,1)} async-done(((bf16[1024,1024]{1,0:T(8,128)(2,1)}), bf16[128,1024]{1,0:T(8,128)(2,1)}) %reduce-scatter.15.cloned.1.call-update) | async-done | bytes 262160 | tf_op jit(solution)/shard_map/reduce_scatter | solution.py:310
  866.6 100.5 %reduce-scatter.19.cloned.1.call-done = bf16[128,4608]{1,0:T(8,128)(2,1)} async-done(((bf16[1024,4608]{1,0:T(8,128)(2,1)}), bf16[128,4608]{1,0:T(8,128)(2,1)}) %reduce-scatter.19.cloned.1.call-update) | async-done | bytes 1179664 | tf_op jit(solution)/shard_map/reduce_scatter | solution.py:316
  967.1 100.1 %reduce-scatter.21.cloned.1.call-done = bf16[128,4608]{1,0:T(8,128)(2,1)} async-done(((bf16[1024,4608]{1,0:T(8,128)(2,1)}), bf16[128,4608]{1,0:T(8,128)(2,1)}) %reduce-scatter.21.cloned.1.call-update) | async-done | bytes 1179664 | tf_op jit(solution)/shard_map/reduce_scatter | solution.py:319
  1067.2 100.0 %reduce-scatter.23.cloned.1.call-done = bf16[576,1024]{1,0:T(8,128)(2,1)} async-done(((bf16[4608,1024]{1,0:T(8,128)(2,1)}), bf16[576,1024]{1,0:T(8,128)(2,1)}) %reduce-scatter.23.cloned.1.call-update) | async-done | bytes 1179664 | tf_op jit(solution)/shard_map/reduce_scatter | solution.py:322
  1168.6 3.5 fusion.82
  1172.1 7.7 fusion.55
  1183.1 13.9 %all-reduce = bf16[2176]{0:T(1024)(128)(2,1)S(1)} all-reduce(bf16[2176]{0:T(1024)(128)(2,1)S(1)} %convert_element_type.230), channel_id=4, replica_groups=mesh['dp'=4,'ctx'=8] {'ctx'}, use_global_device_ids=true, to_apply=%region_24.25.clone | all-reduce | flops 2176 | bytes 8704
  1197.1 9.6 psum.49
  1209.2 68.7 %all-reduce.4.cloned.1.call-done = (bf16[128,1024]{1,0:T(8,128)(2,1)}, bf16[128,1024]{1,0:T(8,128)(2,1)}, bf16[128,1024]{1,0:T(8,128)(2,1)}, bf16[128,4608]{1,0:...) async-done(((bf16[128,1024]{1,0:T(8,128)(2,1)}, bf16[128,1024]{1,0:T(8,128)(2,1)}, bf16[128,1024]{1,0:T(8,128)(2,1)}, bf16[128,4608]{1,0:T(8,128)(2,1)}, ...) | async-done | bytes 4325392 | tf_op jit(solution)/shard_map/psum | solution.py:328
  (525 shorter events, 287.4 us)
Async XLA Ops:
  7.2 40.7 %all-gather.8.cloned.1.call-start = ((), (), s32[]{:S(2)}) async-start(), calls=%async_computation.8 | async-start | bytes 2621440 | tf_op jit(solution)/shard_map/all_gather | solution.py:111
  7.9 77.2 %all-gather.12.cloned.1.call-start = ((), (), s32[]{:S(2)}) async-start(), calls=%async_computation.10 | async-start | bytes 2621440 | tf_op jit(solution)/shard_map/all_gather | solution.py:110
  8.7 125.8 %all-gather.10.cloned.1.call-start = ((), (), s32[]{:S(2)}) async-start(), calls=%async_computation.9 | async-start | bytes 4718592 | tf_op jit(solution)/shard_map/all_gather | solution.py:131
  10.7 37.2 %copy-start.53 = (f32[256]{0:T(256)}, f32[256]{0:T(256)S(1)}, u32[]{:S(2)}) copy-start(f32[256]{0:T(256)S(1)} %get-tuple-element.478) | copy-start | bytes 3076
  11.5 78.1 %copy-start.38 = (f32[256,32]{0,1:T(8,128)}, f32[256,32]{0,1:T(8,128)S(1)}, u32[]{:S(2)}) copy-start(f32[256,32]{0,1:T(8,128)S(1)} %get-tuple-element.469) | copy-start | bytes 98308
  11.5 78.1 %copy-start.40 = (f32[256,32]{0,1:T(8,128)}, f32[256,32]{0,1:T(8,128)S(1)}, u32[]{:S(2)}) copy-start(f32[256,32]{0,1:T(8,128)S(1)} %get-tuple-element.470) | copy-start | bytes 98308
  12.8 37.5 %copy-start.22 = (bf16[256,1024]{1,0:T(8,128)(2,1)}, bf16[256,1024]{1,0:T(8,128)(2,1)S(1)}, u32[]{:S(2)}) copy-start(bf16[256,1024]{1,0:T(8,128)(2,1)S(1)} %fusion.62) | copy-start | bytes 1572868
  54.9 270.6 %all-gather.14.cloned.1.call-start = ((), (), s32[]{:S(2)}) async-start(), calls=%async_computation.11 | async-start | bytes 2621440 | tf_op jit(solution)/shard_map/all_gather | solution.py:112
  55.5 273.8 %all-gather.16.cloned.1.call-start = ((), (), s32[]{:S(2)}) async-start(), calls=%async_computation.12 | async-start | bytes 11796480 | tf_op jit(solution)/shard_map/all_gather | solution.py:113
  56.1 3.8 copy-start.29
  56.1 310.2 %all-gather.18.cloned.1.call-start = ((), (), s32[]{:S(2)}) async-start(), calls=%async_computation.13 | async-start | bytes 11796480 | tf_op jit(solution)/shard_map/all_gather | solution.py:114
  56.7 407.9 %all-gather.20.cloned.1.call-start = ((), (), s32[]{:S(2)}) async-start(), calls=%async_computation.14 | async-start | bytes 11796480 | tf_op jit(solution)/shard_map/all_gather | solution.py:115
  57.5 662.8 %reduce-scatter.9.cloned.1.call-start = ((), (), s32[]{:S(2)}) async-start(), calls=%async_computation.15 | async-start | bytes 2359296 | tf_op jit(solution)/shard_map/reduce_scatter | solution.py:270
  58.4 29.5 %copy-start.34 = (bf16[1,2,128,1024]{3,2,1,0:T(8,128)(2,1)}, bf16[1,2,128,1024]{3,2,1,0:T(8,128)(2,1)S(1)}, u32[]{:S(2)}) copy-start(bf16[1,2,128,1024]{3,2,1,0:T(8,128)(2,1)S(1)} %fusion.60) | copy-start | bytes 1572868
  325.5 3.6 copy-start.52
  474.7 7.0 copy-start.28
  474.7 7.0 copy-start.27
  474.7 7.0 copy-start.10
  474.7 8.5 copy-start.12
  483.2 3.3 copy-start.30
  499.1 6.3 copy-start.3
  505.3 3.3 copy-start
  515.4 5.6 copy-start.4
  521.0 6.3 copy-start.3
  537.8 5.6 copy-start.4
  543.4 6.3 copy-start.3
  560.2 5.6 copy-start.4
  565.8 6.3 copy-start.3
  582.5 5.6 copy-start.4
  588.1 6.2 copy-start.3
  594.3 3.3 copy-start
  604.8 5.6 copy-start.4
  610.4 6.2 copy-start.3
  616.6 3.3 copy-start
  627.1 5.6 copy-start.4
  632.7 6.2 copy-start.3
  638.9 3.3 copy-start
  649.4 5.6 copy-start.4
  655.0 6.2 copy-start.3
  670.9 5.0 copy-start.4
  679.5 5.0 copy-start.16
  684.4 72.6 %reduce-scatter.11.cloned.1.call-start = ((), (), s32[]{:S(2)}) async-start(), calls=%async_computation.16 | async-start | bytes 2359296 | tf_op jit(solution)/shard_map/reduce_scatter | solution.py:273
  686.4 4.6 copy-start.6
  686.4 4.6 copy-start.21
  690.9 102.5 %reduce-scatter.17.cloned.1.call-start = ((), (), s32[]{:S(2)}) async-start(), calls=%async_computation.19 | async-start | bytes 2359296 | tf_op jit(solution)/shard_map/reduce_scatter | solution.py:313
  693.1 137.0 %reduce-scatter.13.cloned.1.call-start = ((), (), s32[]{:S(2)}) async-start(), calls=%async_computation.17 | async-start | bytes 2359296 | tf_op jit(solution)/shard_map/reduce_scatter | solution.py:307
  698.0 168.6 %reduce-scatter.15.cloned.1.call-start = ((), (), s32[]{:S(2)}) async-start(), calls=%async_computation.18 | async-start | bytes 2359296 | tf_op jit(solution)/shard_map/reduce_scatter | solution.py:310
  699.2 22.7 %copy-start.18 = (f32[256,512]{0,1:T(8,128)S(1)}, f32[256,512]{0,1:T(8,128)}, u32[]{:S(2)}) copy-start(f32[256,512]{0,1:T(8,128)} %copy-done.17) | copy-start | bytes 1572868
  721.9 5.9 copy-start.20
  723.7 33.3 %copy-start.23 = (bf16[256,1024]{1,0:T(8,128)(2,1)S(1)}, bf16[256,1024]{1,0:T(8,128)(2,1)}, u32[]{:S(2)}) copy-start(bf16[256,1024]{1,0:T(8,128)(2,1)} %copy-done.22) | copy-start | bytes 1572868
  760.0 207.1 %reduce-scatter.19.cloned.1.call-start = ((), (), s32[]{:S(2)}) async-start(), calls=%async_computation.20 | async-start | bytes 10616832 | tf_op jit(solution)/shard_map/reduce_scatter | solution.py:316
  766.9 300.3 %reduce-scatter.21.cloned.1.call-start = ((), (), s32[]{:S(2)}) async-start(), calls=%async_computation.21 | async-start | bytes 10616832 | tf_op jit(solution)/shard_map/reduce_scatter | solution.py:319
  773.7 393.5 %reduce-scatter.23.cloned.1.call-start = ((), (), s32[]{:S(2)}) async-start(), calls=%async_computation.22 | async-start | bytes 10616832 | tf_op jit(solution)/shard_map/reduce_scatter | solution.py:322
  781.7 385.6 %copy-start.63 = (u32[32]{0:T(128)S(1)}, u32[32]{0:T(128)}, u32[]{:S(2)}) copy-start(u32[32]{0:T(128)} %constant.93) | copy-start | bytes 388
  781.7 386.8 %copy-start.56 = (f32[2,128]{1,0:T(2,128)S(1)}, f32[2,128]{1,0:T(2,128)}, u32[]{:S(2)}) copy-start(f32[2,128]{1,0:T(2,128)} %copy-done.55) | copy-start | bytes 3076
  781.7 386.9 %copy-start.25 = (bf16[256,16,64]{0,2,1:T(8,128)(2,1)S(1)}, bf16[256,16,64]{0,2,1:T(8,128)(2,1)}, u32[]{:S(2)}) copy-start(bf16[256,16,64]{0,2,1:T(8,128)(2,1)} %copy-done.24) | copy-start | bytes 1572868
  781.7 496.2 %all-reduce.4.cloned.1.call-start = ((), (), s32[]{:S(2)}) async-start(), calls=%async_computation.23 | async-start | bytes 8650752 | tf_op jit(solution)/shard_map/psum | solution.py:328
  1167.3 4.8 copy-start.11
  1168.6 3.5 copy-start.26
  1172.1 7.9 copy-start.8
  1172.1 7.9 copy-start.42
  1172.1 7.9 copy-start.50
  1172.1 7.9 copy-start.54
  1282.6 3.4 copy-start.43
  (51 other events, 93.1 us)
Sparse Core Ops, SparseCore 0:
  9.9 38.0 all-gather.7
  49.7 35.2 all-gather.11
  87.3 47.1 all-gather.9
  136.1 34.0 all-gather.13
  171.9 96.3 all-gather.15
  270.0 96.2 all-gather.17
  368.2 96.3 all-gather.19
  684.5 35.7 reduce-scatter.8
  722.6 34.3 reduce-scatter.10
  759.1 34.2 reduce-scatter.16
  795.7 34.3 reduce-scatter.12
  832.2 34.3 reduce-scatter.14
  868.9 98.1 reduce-scatter.18
  969.3 97.8 reduce-scatter.20
  1069.3 97.8 reduce-scatter.22
  1171.4 106.4 all-reduce.3
where the time goes:
time: 1300 us; the launch traced here: 1290 us
  waiting for transfers between devices  728 us (56%)
  matrix products  217 us (17%)
  local copies, waits for them, and re-layouts  168 us (13%)
  other arithmetic  91.8 us (7%)
  loops' own time  47.7 us (4%)
  blocking collectives  23.6 us (2%)
  between operations  16.3 us (1%)
    reduce_scatter x1, waiting for transfers between devices, per_device(): lax.psum_scatter(gate_grad.astype(jnp.bfloat16), 'ctx', scatter_dimension...  100 us
    reduce_scatter x1, waiting for transfers between devices, per_device(): lax.psum_scatter(up_grad.astype(jnp.bfloat16), 'ctx', scatter_dimension=0...  100 us
    reduce_scatter x1, waiting for transfers between devices, per_device(): lax.psum_scatter(down_grad.astype(jnp.bfloat16), 'ctx', scatter_dimension...  100 us
    all_gather x1, waiting for transfers between devices, per_device(): lax.all_gather(down_weight, 'dp', axis=0, tiled=True)  90.3 us
    psum x1, waiting for transfers between devices, per_device(): lax.psum(share_q.astype(jnp.bfloat16), 'dp').astype(jnp.float32)  68.7 us
    all_gather x1, waiting for transfers between devices, per_device(): whole_kv = lax.all_gather(local_kv, 'ctx', axis=1, tiled=True)  44.5 us
    reduce_scatter x1, waiting for transfers between devices, per_device(): lax.psum_scatter(q_grad.astype(jnp.bfloat16), 'ctx', scatter_dimension=0,...  36.7 us
    reduce_scatter x1, waiting for transfers between devices, per_device(): lax.psum_scatter(kv_grad.astype(jnp.bfloat16), 'ctx', scatter_dimension=0...  36.6 us
  transfers between devices with their start and end apart: 16, of which 14 were waited for; matrix products, arithmetic and copies ran while one was open for 20% of the time, Pallas kernels for 0%

commit v1 on v0

--- a/solution.py
+++ b/solution.py
@@ -3,6 +3,8 @@
 import jax
 import jax.numpy as jnp
 from jax import lax
+from jax.experimental import pallas as pl
+from jax.experimental.pallas import tpu as pltpu
 from jax.sharding import PartitionSpec as P
 
 epsilon = 1e-05
@@ -67,6 +69,996 @@
             second_half * cosine - first_half * sine_table,
         ],
         axis=-1,
+    )
+
+
+MESH = pl.DeviceIdType.MESH
+bf16 = jnp.bfloat16
+f32 = jnp.float32
+NEIGHBOURS = (1, 2, 3)
+
+
+def place_of():
+    d = lax.axis_index("dp")
+    ctx = lax.axis_index("ctx")
+    return d, ctx, lax.div(ctx, 2), lax.rem(ctx, 2)
+
+
+def flip(d, k):
+    if k == 0:
+        return d
+    if k == 1:
+        return d + 1 - 2 * lax.rem(d, 2)
+    if k == 2:
+        return lax.rem(d + 2, 4)
+    return 3 - d
+
+
+def nn(a, b):
+    return lax.dot_general(a, b, (((1,), (0,)), ((), ())), preferred_element_type=f32)
+
+
+def nt(a, b):
+    return lax.dot_general(a, b, (((1,), (1,)), ((), ())), preferred_element_type=f32)
+
+
+def tn(a, b):
+    return lax.dot_general(a, b, (((0,), (0,)), ((), ())), preferred_element_type=f32)
+
+
+def exact_nt(a, b):
+    return lax.dot_general(
+        a,
+        b,
+        (((1,), (1,)), ((), ())),
+        preferred_element_type=f32,
+        precision=lax.Precision.HIGHEST,
+    )
+
+
+def lanes(rows):
+    return lax.broadcasted_iota(jnp.int32, (rows, 128), 1)
+
+
+def head_sum(u):
+    low = lanes(u.shape[0]) < 64
+    first = jnp.sum(jnp.where(low, u, 0.0), axis=-1, keepdims=True)
+    second = jnp.sum(jnp.where(low, 0.0, u), axis=-1, keepdims=True)
+    return jnp.where(low, first, second)
+
+
+def half_turn(u):
+    first = lax.rem(lanes(u.shape[0]), 64) < 32
+    return jnp.where(first, pltpu.roll(u, 96, 1), pltpu.roll(u, 32, 1))
+
+
+def head_marks(chunk):
+    head = lax.broadcasted_iota(jnp.int32, (16, 128), 0)
+    column = lax.broadcasted_iota(jnp.int32, (16, 128), 1) + 128 * chunk
+    return (lax.div(column, 64) == head).astype(f32)
+
+
+class Gather:
+    def __init__(self, buf, send, recv, row0, rows, index, share=False, row0_other=None):
+        self.buf, self.send, self.recv = buf, send, recv
+        self.row0, self.rows, self.index = row0, rows, index
+        self.share, self.row0_other = share, row0_other
+        self.d, self.ctx, self.z, self.c = place_of()
+
+    def device(self, j):
+        if j == 4:
+            return (self.d, 2 * self.z + 1 - self.c)
+        return (flip(self.d, j), self.ctx)
+
+    def where(self, k, j):
+        if self.index == "absolute":
+            return flip(self.d, k)
+        return k if j == 4 else k ^ j
+
+    def copy(self, slot, k, j, row0, rows):
+        source = self.buf.at[self.where(k, 0), pl.ds(row0, rows)]
+        return pltpu.make_async_remote_copy(
+            src_ref=source,
+            dst_ref=self.buf.at[self.where(k, j), pl.ds(row0, rows)],
+            send_sem=self.send.at[slot],
+            recv_sem=self.recv.at[slot],
+            device_id=self.device(j),
+            device_id_type=MESH,
+        )
+
+    def plan(self):
+        half = self.rows // 2
+        first, second = self.row0, self.row0 + half
+        steps = [
+            (0, 0, 1, self.row0, self.rows),
+            (1, 0, 2, self.row0, self.rows),
+            (2, 1, 2, first, half),
+            (3, 2, 1, second, half),
+        ]
+        if self.share:
+            steps += [
+                (4, 1, 4, self.row0, self.rows),
+                (5, 2, 4, self.row0, self.rows),
+                (6, 3, 4, first, half),
+                (7, 3, 4, second, half),
+            ]
+        return steps
+
+    def begin(self, slot):
+        self.copy(*self.plan()[slot]).start()
+
+    def landed(self, slot):
+        half = self.rows // 2
+        other = self.row0_other
+        k, row0, rows = [
+            (1, self.row0, self.rows),
+            (2, self.row0, self.rows),
+            (3, self.row0, half),
+            (3, self.row0 + half, half),
+            (1, other, self.rows),
+            (2, other, self.rows),
+            (3, other, half),
+            (3, (other + half) if other is not None else None, half),
+        ][slot]
+        block = self.buf.at[self.where(k, 0), pl.ds(row0, rows)]
+        pltpu.make_async_remote_copy(
+            src_ref=block,
+            dst_ref=block,
+            send_sem=self.send.at[slot],
+            recv_sem=self.recv.at[slot],
+            device_id=self.device(1),
+            device_id_type=MESH,
+        ).wait_recv()
+
+    def start(self):
+        self.begin(0)
+        self.begin(1)
+
+    def hop_near(self):
+        self.landed(0)
+        self.begin(2)
+        if self.share:
+            self.begin(4)
+        self.landed(1)
+        self.begin(3)
+        if self.share:
+            self.begin(5)
+
+    def hop_far(self):
+        self.landed(2)
+        if self.share:
+            self.begin(6)
+        self.landed(3)
+        if self.share:
+            self.begin(7)
+
+    def drain(self):
+        for step in self.plan():
+            self.copy(*step).wait_send()
+
+
+def greet(plane, sibling, z_near, z_far):
+    d, ctx, z, c = place_of()
+    barrier = pltpu.get_barrier_semaphore()
+    count = 0
+
+    def call(dp, other):
+        pl.semaphore_signal(barrier, inc=1, device_id=(dp, other), device_id_type=MESH)
+
+    for k in plane:
+        call(flip(d, k), ctx)
+        count += 1
+    if sibling:
+        call(d, 2 * z + 1 - c)
+        count += 1
+    if z_near == "line":
+
+        @pl.when(z > 0)
+        def _():
+            call(d, ctx - 2)
+
+        @pl.when(z < 3)
+        def _():
+            call(d, ctx + 2)
+
+        count = count + jnp.where(z > 0, 1, 0) + jnp.where(z < 3, 1, 0)
+    if z_near == "pair":
+        call(d, 2 * flip(z, 1) + c)
+        count += 1
+    if z_far:
+        call(d, 2 * flip(z, 2) + c)
+        count += 1
+    return barrier, count
+
+
+def front_kernel(
+    x_ref, norm_ref, qw_ref, kvw_ref, outw_ref, gate_ref, up_ref, dffn_ref, cos_ref, sin_ref, qg_ref,
+    kg_ref, qpos_ref, kpos_ref,
+    h1_ref, raw_ref, qp_ref, kv_ref, ob_ref, o_ref, lrow_ref, w_ref, wout_ref, gu_ref, dall_ref,
+    acc_ref, sum_ref, bias_ref,
+    loc, wsend, wrecv, osend, orecv, dsend, drecv, gsend, grecv, lsend, lrecv, ssend, srecv,
+):
+    d, ctx, z, c = place_of()
+    sibling = (d, 2 * z + 1 - c)
+    slice_width = gu_ref.shape[3]
+    barrier, count = greet((1, 2, 3), True, "line", False)
+
+    def local(source, target, slot):
+        return pltpu.make_async_copy(source, target, loc.at[slot])
+
+    own = [
+        local(qw_ref, w_ref.at[d, :, pl.ds(0, 1024)], 0),
+        local(kvw_ref, w_ref.at[d, :, pl.ds(1024, 1024)], 1),
+        local(outw_ref, wout_ref.at[d], 2),
+        local(dffn_ref, dall_ref.at[0], 3),
+        local(gate_ref.at[:, pl.ds(pl.multiple_of(d * slice_width, 128), slice_width)], gu_ref.at[0, d], 4),
+        local(up_ref.at[:, pl.ds(pl.multiple_of(d * slice_width, 128), slice_width)], gu_ref.at[1, d], 5),
+    ]
+    for copy in own:
+        copy.start()
+
+    x = x_ref[...].astype(f32)
+    scale = lax.rsqrt(jnp.mean(x * x, axis=-1, keepdims=True) + epsilon)
+    h1_ref[...] = (x * scale * norm_ref[...]).astype(bf16)
+    own[0].wait()
+    own[1].wait()
+    pl.semaphore_wait(barrier, count)
+
+    half = 128
+    qkv = Gather(w_ref, wsend, wrecv, half * c, half, "absolute", True, half * (1 - c))
+    wout = Gather(wout_ref, osend, orecv, half * c, half, "absolute", True, half * (1 - c))
+    dall = Gather(dall_ref, dsend, drecv, 0, 256, "relative")
+
+    def multiply(k, first):
+        e = flip(d, k)
+        part = nn(h1_ref[:, pl.ds(pl.multiple_of(e * 256, 256), 256)], w_ref[e])
+        acc_ref[...] = part if first else acc_ref[...] + part
+
+    qkv.start()
+    multiply(0, True)
+    qkv.hop_near()
+    own[2].wait()
+    own[3].wait()
+    qkv.landed(4)
+    multiply(1, False)
+    qkv.landed(5)
+    multiply(2, False)
+    qkv.hop_far()
+
+    def spread(wait):
+        for j in NEIGHBOURS:
+            for core, weight in ((0, gate_ref), (1, up_ref)):
+
+                @pl.when(c == core)
+                def _():
+                    copy = pltpu.make_async_remote_copy(
+                        src_ref=weight.at[
+                            :, pl.ds(pl.multiple_of(flip(d, j) * slice_width, 128), slice_width)
+                        ],
+                        dst_ref=gu_ref.at[core, d],
+                        send_sem=gsend.at[j - 1],
+                        recv_sem=grecv.at[j - 1],
+                        device_id=(flip(d, j), ctx),
+                        device_id_type=MESH,
+                    )
+                    if wait:
+                        copy.wait_send()
+                    else:
+                        copy.start()
+
+    def spread_on(j):
+        return pltpu.make_async_remote_copy(
+            src_ref=gu_ref.at[c, flip(d, j)],
+            dst_ref=gu_ref.at[c, flip(d, j)],
+            send_sem=gsend.at[j + 2],
+            recv_sem=grecv.at[j + 2],
+            device_id=sibling,
+            device_id_type=MESH,
+        )
+
+    def spread_landed(slot, core, j):
+        pltpu.make_async_remote_copy(
+            src_ref=gu_ref.at[core, flip(d, j)],
+            dst_ref=gu_ref.at[core, flip(d, j)],
+            send_sem=gsend.at[slot],
+            recv_sem=grecv.at[slot],
+            device_id=sibling,
+            device_id_type=MESH,
+        ).wait_recv()
+
+    wout.start()
+    dall.start()
+    spread(False)
+    qkv.landed(6)
+    qkv.landed(7)
+    multiply(3, False)
+
+    cosine, sine = cos_ref[...], sin_ref[...]
+    low = lanes(256) < 64
+
+    def turned(u, gain):
+        normed = u * lax.rsqrt(head_sum(u * u) * (1.0 / 64) + epsilon) * gain
+        return normed * cosine + half_turn(normed) * sine
+
+    for m in range(4):
+        u = acc_ref[:, 1024 + 128 * m : 1152 + 128 * m]
+        kv_ref[ctx, :, 128 * m : 128 * (m + 1)] = turned(u, kg_ref[...]).astype(bf16)
+    kv_ref[ctx, :, 512:] = acc_ref[:, 1536:].astype(bf16)
+
+    def line_copy(slot, block, target):
+        return pltpu.make_async_remote_copy(
+            src_ref=kv_ref.at[block],
+            dst_ref=kv_ref.at[block],
+            send_sem=lsend.at[slot],
+            recv_sem=lrecv.at[slot],
+            device_id=(d, target),
+            device_id_type=MESH,
+        )
+
+    def sibling_line(slot, block):
+        return pltpu.make_async_remote_copy(
+            src_ref=kv_ref.at[block],
+            dst_ref=kv_ref.at[block],
+            send_sem=lsend.at[slot],
+            recv_sem=lrecv.at[slot],
+            device_id=sibling,
+            device_id_type=MESH,
+        )
+
+    def sibling_copy(slot, block):
+        return pltpu.make_async_remote_copy(
+            src_ref=kv_ref.at[block],
+            dst_ref=kv_ref.at[block],
+            send_sem=ssend.at[slot],
+            recv_sem=srecv.at[slot],
+            device_id=sibling,
+            device_id_type=MESH,
+        )
+
+    @pl.when(z < 3)
+    def _():
+        line_copy(1, ctx, ctx + 2).start()
+
+    @pl.when(z > 0)
+    def _():
+        line_copy(2, ctx, ctx - 2).start()
+
+    sibling_copy(0, ctx).start()
+
+    for n in range(8):
+        u = turned(acc_ref[:, 128 * n : 128 * (n + 1)], qg_ref[...])
+        other = pltpu.roll(u, 64, 1)
+        if n % 2 == 0:
+            even, odd = jnp.where(low, u, 0.0), jnp.where(low, other, 0.0)
+        else:
+            even, odd = jnp.where(low, 0.0, other), jnp.where(low, 0.0, u)
+        qp_ref[n, 0:256] = even.astype(bf16)
+        qp_ref[n, 256:512] = odd.astype(bf16)
+    raw_ref[...] = acc_ref[:, 0:1536]
+
+    sum_ref[...] = jnp.zeros_like(sum_ref)
+    ones = jnp.ones((256, 128), bf16)
+    to_exponent = math.log2(math.e) / 8.0
+
+    def attend(block):
+        bias_ref[...] = jnp.where(kpos_ref[block] <= qpos_ref[...], 0.0, masked_score)
+
+        def head(n, _):
+            m = lax.div(n, 2)
+            keys = kv_ref[block, :, pl.ds(pl.multiple_of(128 * m, 128), 128)]
+            values = kv_ref[block, :, pl.ds(pl.multiple_of(512 + 128 * m, 128), 128)]
+            scores = nt(qp_ref[n], keys) * to_exponent
+            bias = bias_ref[...]
+            terms = jnp.concatenate(
+                [jnp.exp2(scores[0:256] + bias), jnp.exp2(scores[256:512] + bias)], axis=0
+            ).astype(bf16)
+            sum_ref[n] += nn(terms, jnp.concatenate([values, ones], axis=1))
+            return 0
+
+        lax.fori_loop(0, 8, head, 0)
+
+    def step(j, _):
+        k = lax.div(j + 1, 2)
+        side = lax.rem(j + 1, 2)
+        toward = jnp.where(j == 0, 0, 1 - 2 * side)
+        source = z - toward * k
+
+        @pl.when((source >= 0) & (source <= 3))
+        def _():
+            block = 2 * source + c
+            target = z + toward
+
+            @pl.when(j > 0)
+            def _():
+                sibling_line(j, block).wait_recv()
+
+                @pl.when((target >= 0) & (target <= 3))
+                def _():
+                    line_copy(j + 2, block, 2 * target + c).start()
+
+                sibling_copy(j, block).start()
+
+            attend(block)
+            mate = 2 * source + 1 - c
+            sibling_copy(j, mate).wait_recv()
+            attend(mate)
+
+        @pl.when(j == 0)
+        def _():
+            wout.hop_near()
+
+        @pl.when(j == 2)
+        def _():
+            wout.hop_far()
+            dall.hop_near()
+
+        return 0
+
+    lax.fori_loop(0, 7, step, 0)
+    for n in range(8):
+        total = sum_ref[n]
+        weight = total[:, 128:]
+        part = total[:, :128] / weight
+        even, odd = part[0:256], part[256:512]
+        if n % 2 == 0:
+            chunk = jnp.where(low, even, pltpu.roll(odd, 64, 1))
+        else:
+            chunk = jnp.where(low, pltpu.roll(even, 64, 1), odd)
+        o_ref[:, 128 * n : 128 * (n + 1)] = chunk
+        ob_ref[:, 128 * n : 128 * (n + 1)] = chunk.astype(bf16)
+        whole = jnp.where(low, weight[0:256], weight[256:512])
+        rows = exact_nt(head_marks(n), jnp.log2(whole)) * (1.0 / 64)
+        lrow_ref[...] = rows if n == 0 else lrow_ref[...] + rows
+
+    def line_drain(j, _):
+        k = lax.div(j + 1, 2)
+        side = lax.rem(j + 1, 2)
+        toward = jnp.where(j == 0, 0, 1 - 2 * side)
+        source = z - toward * k
+
+        @pl.when((source >= 0) & (source <= 3))
+        def _():
+            block = 2 * source + c
+            target = z + toward
+            sibling_copy(j, block).wait_send()
+
+            @pl.when((j > 0) & (target >= 0) & (target <= 3))
+            def _():
+                line_copy(j + 2, block, 2 * target + c).wait_send()
+
+        return 0
+
+    lax.fori_loop(0, 7, line_drain, 0)
+
+    @pl.when(z < 3)
+    def _():
+        line_copy(1, ctx, ctx + 2).wait_send()
+
+    @pl.when(z > 0)
+    def _():
+        line_copy(2, ctx, ctx - 2).wait_send()
+
+    dall.hop_far()
+    for j in NEIGHBOURS:
+        spread_landed(j - 1, c, j)
+        spread_on(j).start()
+    for slot in (4, 5, 6, 7):
+        wout.landed(slot)
+    for j in NEIGHBOURS:
+        spread_landed(j + 2, 1 - c, j)
+        spread_on(j).wait_send()
+    spread(True)
+    qkv.drain()
+    wout.drain()
+    dall.drain()
+    own[4].wait()
+    own[5].wait()
+
+
+def vmem():
+    return pl.BlockSpec(memory_space=pltpu.VMEM)
+
+
+def anywhere():
+    return pl.BlockSpec(memory_space=pl.ANY)
+
+
+def shape(dims, dtype):
+    return jax.ShapeDtypeStruct(dims, dtype)
+
+
+def sems(n):
+    return pltpu.SemaphoreType.DMA((n,))
+
+
+def front(x, norm_in, q_weight, kv_weight, out_weight, gate_weight, up_weight, dffn, cosine, sine, q_gain, k_gain, qpos, kpos):
+    width = gate_weight.shape[1] // 4
+    return pl.pallas_call(
+        front_kernel,
+        out_shape=(
+            shape((256, 1024), bf16),
+            shape((256, 1536), f32),
+            shape((8, 512, 128), bf16),
+            shape((8, 256, 1024), bf16),
+            shape((256, 1024), bf16),
+            shape((256, 1024), f32),
+            shape((16, 256), f32),
+            shape((4, 256, 2048), bf16),
+            shape((4, 256, 1024), bf16),
+            shape((2, 4, 256, width), bf16),
+            shape((4, 256, 1024), bf16),
+        ),
+        in_specs=[vmem(), vmem()] + [anywhere()] * 6 + [vmem()] * 6,
+        out_specs=[vmem()] * 11,
+        scratch_shapes=[
+            pltpu.VMEM((256, 2048), f32),
+            pltpu.VMEM((8, 512, 256), f32),
+            pltpu.VMEM((256, 256), f32),
+            sems(6),
+            sems(8), sems(8), sems(8), sems(8), sems(4), sems(4), sems(6), sems(6), sems(9), sems(9), sems(7), sems(7),
+        ],
+        compiler_params=pltpu.CompilerParams(collective_id=1, has_side_effects=True, vmem_limit_bytes=56 * 2**20),
+        name="front",
+    )(x, norm_in, q_weight, kv_weight, out_weight, gate_weight, up_weight, dffn, cosine, sine, q_gain, k_gain, qpos, kpos)
+
+
+def remote(source, target, send, recv, device):
+    return pltpu.make_async_remote_copy(
+        src_ref=source, dst_ref=target, send_sem=send, recv_sem=recv, device_id=device, device_id_type=MESH
+    )
+
+
+def total(*refs):
+    out = refs[0][...].astype(f32)
+    for ref in refs[1:]:
+        out = out + ref[...].astype(f32)
+    return out
+
+
+class CtxSum:
+    def __init__(self, chunk, core_in, near_in, far_in, send, recv):
+        self.chunk, self.core_in, self.near_in, self.far_in = chunk, core_in, near_in, far_in
+        self.send, self.recv = send, recv
+        self.d, self.ctx, self.z, self.c = place_of()
+
+    def core_copy(self, r):
+        return remote(
+            self.chunk(r, 1 - self.c),
+            self.core_in.at[r],
+            self.send.at[r],
+            self.recv.at[r],
+            (self.d, 2 * self.z + 1 - self.c),
+        )
+
+    def near_copy(self, r):
+        slot = 0 if r == 3 else 1
+        return remote(
+            self.chunk(r, self.c),
+            self.near_in.at[slot],
+            self.send.at[4 + slot],
+            self.recv.at[4 + slot],
+            (self.d, 2 * flip(self.z, 1) + self.c),
+        )
+
+    def far_copy(self):
+        return remote(
+            self.chunk(2, self.c),
+            self.far_in,
+            self.send.at[6],
+            self.recv.at[6],
+            (self.d, 2 * flip(self.z, 2) + self.c),
+        )
+
+    def begin(self, r):
+        self.core_copy(r).start()
+
+    def add_core(self, r):
+        self.core_copy(r).wait_recv()
+        mine = self.chunk(r, self.c)
+        mine[...] = total(mine, self.core_in.at[r]).astype(bf16)
+
+    def pass_near(self, r):
+        self.near_copy(r).start()
+
+    def pass_far(self):
+        self.near_copy(3).wait_recv()
+        mine = self.chunk(2, self.c)
+        mine[...] = total(mine, self.near_in.at[0]).astype(bf16)
+        self.far_copy().start()
+
+    def result(self):
+        self.near_copy(1).wait_recv()
+        self.far_copy().wait_recv()
+        return total(self.chunk(0, self.c), self.near_in.at[1], self.far_in)
+
+    def drain_core(self):
+        for r in range(4):
+            self.core_copy(r).wait_send()
+
+    def drain(self, core=True):
+        if core:
+            self.drain_core()
+        self.near_copy(3).wait_send()
+        self.near_copy(1).wait_send()
+        self.far_copy().wait_send()
+
+
+def middle_kernel(
+    x_ref, ob_ref, o_ref, lrow_ref, nmid_ref, qpos_ref, kpos_ref, wout_ref, gu_hbm, down_hbm, dall_hbm, kv_hbm, qp_hbm,
+    y_ref, dy_ref, dattn_ref, gmid_ref, dq_ref, dkv_ref, gate_ref, up_ref, downg_ref,
+    gu, down, dall, kv, qp, h2, act, y1, own_y, own_p, y_out, p_out, y_in, p_in,
+    dop, dqt, bias, core_in, near_in, far_in, dcore, dsum, dnear, dfar, kcore, knear, kfar,
+    loc, hsend, hrecv, psend, precv, ysend, yrecv, gsend, grecv, usend, urecv, dsend, drecv, asend, arecv, ksend, krecv,
+):
+    d, ctx, z, c = place_of()
+    sibling = (d, 2 * z + 1 - c)
+    width = act.shape[2]
+    barrier, count = greet((1, 2, 3), True, "pair", True)
+    loads = [
+        pltpu.make_async_copy(source, target, loc.at[slot])
+        for slot, (source, target) in enumerate(
+            ((gu_hbm, gu), (down_hbm, down), (dall_hbm, dall), (kv_hbm, kv), (qp_hbm, qp))
+        )
+    ]
+    for copy in loads:
+        copy.start()
+
+    residual = x_ref[...].astype(f32) + nn(ob_ref[...], wout_ref[...])
+    y1[...] = residual
+    scale = lax.rsqrt(jnp.mean(residual * residual, axis=-1, keepdims=True) + epsilon)
+    h2[0] = (residual * scale * nmid_ref[...]).astype(bf16)
+    pl.semaphore_wait(barrier, count)
+    gather = Gather(h2, hsend, hrecv, 0, 256, "relative")
+    gather.start()
+    for copy in loads[:3]:
+        copy.wait()
+
+    def ffn(first, blocks):
+        rows = 256 * blocks
+        span = slice(first * 256, first * 256 + rows)
+        tokens = h2[first : first + blocks].reshape(rows, 1024)
+        grads = dall[first : first + blocks].reshape(rows, 1024)
+        gate = nn(tokens, gu[0])
+        up = nn(tokens, gu[1])
+        sig = jax.nn.sigmoid(gate)
+        silu = gate * sig
+        act[0, span, :] = (silu * up).astype(bf16)
+        dact = nt(grads, down[...])
+        act[1, span, :] = (dact * up * sig * (1.0 + gate * (1.0 - sig))).astype(bf16)
+        act[2, span, :] = (dact * silu).astype(bf16)
+        part = nt(act[1, span, :], gu[0]) + nt(act[2, span, :], gu[1])
+        if first == 0:
+            own_p[...] = part
+        else:
+            p_out[first - 1 : first - 1 + blocks] = part.astype(bf16).reshape(blocks, 256, 1024)
+        return span
+
+    def ffn_out(first, blocks):
+        span = slice(first * 256, first * 256 + 256 * blocks)
+        part = nn(act[0, span, :], down[...])
+        if first == 0:
+            own_y[...] = part
+        else:
+            y_out[first - 1 : first - 1 + blocks] = part.astype(bf16).reshape(blocks, 256, 1024)
+
+    def scatter(out_buf, in_buf, send, recv, k):
+        return remote(out_buf.at[k - 1], in_buf.at[k - 1], send.at[k - 1], recv.at[k - 1], (flip(d, k), ctx))
+
+    ffn(0, 1)
+    gather.hop_near()
+    ffn(1, 2)
+    scatter(p_out, p_in, psend, precv, 1).start()
+    scatter(p_out, p_in, psend, precv, 2).start()
+    gather.hop_far()
+    ffn(3, 1)
+    scatter(p_out, p_in, psend, precv, 3).start()
+    ffn_out(0, 1)
+    ffn_out(1, 2)
+    ffn_out(3, 1)
+    for k in NEIGHBOURS:
+        scatter(y_out, y_in, ysend, yrecv, k).start()
+
+    tokens = h2[...].reshape(1024, 1024)
+    down[...] = tn(act[0], dall[...].reshape(1024, 1024)).astype(bf16)
+    half = down.shape[0] // 2
+
+    def down_core():
+        return remote(down.at[pl.ds(half * (1 - c), half)], dcore, dsend.at[0], drecv.at[0], sibling)
+
+    down_core().start()
+    gu[0] = tn(tokens, act[1]).astype(bf16)
+
+    def weight_sum(t, send, recv):
+        return CtxSum(
+            lambda r, core: gu.at[t, pl.ds(128 * (2 * flip(z, r) + core), 128)],
+            core_in.at[t],
+            near_in.at[t],
+            far_in.at[t],
+            send,
+            recv,
+        )
+
+    gate_sum = weight_sum(0, gsend, grecv)
+    up_sum = weight_sum(1, usend, urecv)
+    for r in (3, 1, 2, 0):
+        gate_sum.begin(r)
+    gu[1] = tn(tokens, act[2]).astype(bf16)
+    for r in (3, 1, 2, 0):
+        up_sum.begin(r)
+
+    down_core().wait_recv()
+
+    def down_piece(j):
+        return down.at[pl.ds(half * c, half), pl.ds(pl.multiple_of(256 * flip(d, j), 256), 256)]
+
+    down_mine = down.at[pl.ds(half * c, half)]
+    down_mine[...] = total(down_mine, dcore).astype(bf16)
+
+    def down_copy(j):
+        return remote(down_piece(j), dsum.at[d], dsend.at[j], drecv.at[j], (flip(d, j), ctx))
+
+    def down_landed(j):
+        piece = dsum.at[flip(d, j)]
+        remote(piece, piece, dsend.at[j], drecv.at[j], (flip(d, j), ctx)).wait_recv()
+
+    for j in NEIGHBOURS:
+        down_copy(j).start()
+    dsum[d] = down_piece(0)[...]
+
+    def part_sum(item, rs):
+        for r in rs:
+            item.add_core(r)
+            if r in (1, 3):
+                item.pass_near(r)
+
+    part_sum(gate_sum, (3, 1, 2, 0))
+    part_sum(up_sum, (3, 1, 2, 0))
+
+    dmid = own_p[...]
+    for k in NEIGHBOURS:
+        scatter(p_out, p_in, psend, precv, k).wait_recv()
+        dmid = dmid + p_in[k - 1].astype(f32)
+    residual = y1[...]
+    scale = lax.rsqrt(jnp.mean(residual * residual, axis=-1, keepdims=True) + epsilon)
+    gmid_ref[...] = jnp.sum(dmid * residual * scale, axis=0, keepdims=True)
+    scaled = dmid * nmid_ref[...]
+    dy = dall[0].astype(f32) + scale * scaled - residual * (scale * scale * scale) * jnp.mean(
+        scaled * residual, axis=-1, keepdims=True
+    )
+    dy_ref[...] = dy
+    dattn = dy.astype(bf16)
+    dattn_ref[...] = dattn
+    d_mixed = nt(dattn, wout_ref[...])
+    low = lanes(256) < 64
+    delta = None
+    for n in range(8):
+        u = d_mixed[:, 128 * n : 128 * (n + 1)].astype(bf16).astype(f32)
+        other = pltpu.roll(u, 64, 1)
+        if n % 2 == 0:
+            even, odd = jnp.where(low, u, 0.0), jnp.where(low, other, 0.0)
+        else:
+            even, odd = jnp.where(low, 0.0, other), jnp.where(low, 0.0, u)
+        dop[n, 0:256] = even.astype(bf16)
+        dop[n, 256:512] = odd.astype(bf16)
+        rows = exact_nt(head_marks(n), u * o_ref[:, 128 * n : 128 * (n + 1)])
+        delta = rows if delta is None else delta + rows
+
+    loads[3].wait()
+    loads[4].wait()
+    to_exponent = math.log2(math.e) / 8.0
+    dqt[...] = jnp.zeros_like(dqt)
+
+    def dkv_chunk(r, core):
+        block = 2 * flip(z, r) + core
+        return act.at[lax.div(block, 4), pl.ds(256 * lax.rem(block, 4), 256), pl.ds(0, 1024)]
+
+    dkv_sum = CtxSum(dkv_chunk, kcore, knear, kfar, ksend, krecv)
+
+    def row_of(table, m):
+        return jnp.concatenate([table[4 * m + i : 4 * m + i + 1, :] for i in range(4)], axis=1)
+
+    lrow = lrow_ref[...]
+
+    def attend_back(block, target):
+        bias[...] = jnp.where(kpos_ref[block] <= qpos_ref[...], 0.0, masked_score)
+        for m in range(4):
+            keys = kv[block, :, 128 * m : 128 * (m + 1)]
+            values = kv[block, :, 512 + 128 * m : 512 + 128 * (m + 1)]
+            queries = qp[2 * m : 2 * m + 2].reshape(1024, 128)
+            grads = dop[2 * m : 2 * m + 2].reshape(1024, 128)
+            scores = nt(keys, queries) * to_exponent - row_of(lrow, m)
+            weights = jnp.concatenate(
+                [jnp.exp2(scores[:, 256 * i : 256 * (i + 1)] + bias[...]) for i in range(4)], axis=1
+            )
+            dweights = nt(values, grads)
+            dscores = (weights * (dweights - row_of(delta, m))).astype(bf16)
+            target[:, 128 * m : 128 * (m + 1)] = (nn(dscores, queries) * 0.125).astype(bf16)
+            target[:, 512 + 128 * m : 512 + 128 * (m + 1)] = nn(weights.astype(bf16), grads).astype(bf16)
+            dqt[m] += tn(keys, dscores)
+
+    for r in (3, 1, 2, 0):
+        for core in (0, 1):
+            attend_back(2 * flip(z, r) + core, dkv_chunk(r, core))
+        dkv_sum.begin(r)
+        dkv_sum.add_core(r)
+        if r in (1, 3):
+            dkv_sum.pass_near(r)
+        if r == 3:
+            gate_sum.pass_far()
+        if r == 1:
+            up_sum.pass_far()
+        if r == 2:
+            for j in NEIGHBOURS:
+                down_landed(j)
+
+    down_sum = CtxSum(
+        lambda r, core: dsum.at[flip(z, r)], None, dnear, dfar, asend, arecv
+    )
+    down_sum.pass_near(3)
+    down_sum.pass_near(1)
+    for n in range(8):
+        m, e = n // 2, n % 2
+        turned = dqt[m, :, 512 * e : 512 * (e + 1)].T
+        even, odd = turned[0:256], turned[256:512]
+        if e == 0:
+            chunk = jnp.where(low, even, pltpu.roll(odd, 64, 1))
+        else:
+            chunk = jnp.where(low, pltpu.roll(even, 64, 1), odd)
+        dq_ref[:, 128 * n : 128 * (n + 1)] = chunk * 0.125
+    dkv_sum.pass_far()
+    down_sum.pass_far()
+    gate_ref[...] = gate_sum.result().astype(bf16)
+    up_ref[...] = up_sum.result().astype(bf16)
+    out = y1[...] + own_y[...]
+    for k in NEIGHBOURS:
+        scatter(y_out, y_in, ysend, yrecv, k).wait_recv()
+        out = out + y_in[k - 1].astype(f32)
+    y_ref[...] = out.astype(bf16)
+    dkv_ref[...] = dkv_sum.result()
+    downg_ref[...] = down_sum.result().astype(bf16)
+
+    gather.drain()
+    for k in NEIGHBOURS:
+        scatter(p_out, p_in, psend, precv, k).wait_send()
+        scatter(y_out, y_in, ysend, yrecv, k).wait_send()
+        down_copy(k).wait_send()
+    down_core().wait_send()
+    gate_sum.drain()
+    up_sum.drain()
+    down_sum.drain(core=False)
+    dkv_sum.drain()
+
+
+def middle(x, ob, o, lrow, norm_mid, qpos, kpos, wout, gu, down, dall, kv, qp):
+    width = gu.shape[2]
+    half = width // 2
+    return pl.pallas_call(
+        middle_kernel,
+        out_shape=(
+            shape((256, 1024), bf16),
+            shape((256, 1024), f32),
+            shape((256, 1024), bf16),
+            shape((1, 1024), f32),
+            shape((256, 1024), f32),
+            shape((256, 1024), f32),
+            shape((128, width), bf16),
+            shape((128, width), bf16),
+            shape((half, 256), bf16),
+        ),
+        in_specs=[vmem()] * 8 + [anywhere()] * 5,
+        out_specs=[vmem()] * 9,
+        scratch_shapes=[
+            pltpu.VMEM((2, 1024, width), bf16),
+            pltpu.VMEM((width, 1024), bf16),
+            pltpu.VMEM((4, 256, 1024), bf16),
+            pltpu.VMEM((8, 256, 1024), bf16),
+            pltpu.VMEM((8, 512, 128), bf16),
+            pltpu.VMEM((4, 256, 1024), bf16),
+            pltpu.VMEM((3, 1024, width), bf16),
+            pltpu.VMEM((256, 1024), f32),
+            pltpu.VMEM((256, 1024), f32),
+            pltpu.VMEM((256, 1024), f32),
+            pltpu.VMEM((3, 256, 1024), bf16),
+            pltpu.VMEM((3, 256, 1024), bf16),
+            pltpu.VMEM((3, 256, 1024), bf16),
+            pltpu.VMEM((3, 256, 1024), bf16),
+            pltpu.VMEM((8, 512, 128), bf16),
+            pltpu.VMEM((4, 128, 1024), f32),
+            pltpu.VMEM((256, 256), f32),
+            pltpu.VMEM((2, 4, 128, width), bf16),
+            pltpu.VMEM((2, 2, 128, width), bf16),
+            pltpu.VMEM((2, 128, width), bf16),
+            pltpu.VMEM((half, 1024), bf16),
+            pltpu.VMEM((4, half, 256), bf16),
+            pltpu.VMEM((2, half, 256), bf16),
+            pltpu.VMEM((half, 256), bf16),
+            pltpu.VMEM((4, 256, 1024), bf16),
+            pltpu.VMEM((2, 256, 1024), bf16),
+            pltpu.VMEM((256, 1024), bf16),
+            sems(5), sems(4), sems(4), sems(3), sems(3), sems(3), sems(3), sems(7), sems(7), sems(7), sems(7),
+            sems(4), sems(4), sems(7), sems(7), sems(7), sems(7),
+        ],
+        compiler_params=pltpu.CompilerParams(collective_id=2, has_side_effects=True, vmem_limit_bytes=62 * 2**20),
+        name="middle",
+    )(x, ob, o, lrow, norm_mid, qpos, kpos, wout, gu, down, dall, kv, qp)
+
+
+def staged(
+    hidden_in, cotangent, lengths, block_map, norm_in, q_weight, kv_weight, q_gain, k_gain, out_weight,
+    norm_mid, gate_weight, up_weight, down_weight,
+):
+    block_size = hidden_in.shape[2]
+    width = hidden_in.shape[3]
+    head_size = q_gain.shape[0]
+    ctx_count = lax.axis_size("ctx")
+    offsets = jnp.arange(block_size, dtype=jnp.int32)
+    own_blocks = lax.dynamic_slice_in_dim(block_map, lax.axis_index("ctx") * 2, 2)
+    query_pos = (own_blocks[:, None] * block_size + offsets[None, :]).reshape(-1)
+    key_pos = (block_map[:, None] * block_size + offsets[None, :]).reshape(-1)
+    key_pos = jnp.where(key_pos < lengths[0], key_pos, jnp.int32(2**30))
+    tokens = query_pos.shape[0]
+    cosine, sine_table = tables(query_pos, head_size)
+    cos_wide = jnp.tile(cosine[:, 0, :], (1, 4))
+    sin_wide = jnp.tile(jnp.concatenate([-sine_table[:, 0, :], sine_table[:, 0, :]], axis=1), (1, 2))
+    x = hidden_in.reshape(tokens, width)
+    valid = (query_pos < lengths[0])[:, None]
+    dffn = jnp.where(valid, cotangent.reshape(tokens, width), jnp.zeros((), bf16))
+    h1, raw, qp, kv, ob, o, lrow, w, wout, gu, dall = front(
+        x, norm_in[None], q_weight, kv_weight, out_weight, gate_weight, up_weight, dffn, cos_wide, sin_wide,
+        jnp.tile(q_gain, 2)[None], jnp.tile(k_gain, 2)[None], query_pos[:, None], key_pos.reshape(ctx_count, 1, -1),
+    )
+    y, dy, dattn, gmid, dq, dkv, gate_piece, up_piece, down_piece = middle(
+        x, ob, o, lrow, norm_mid[None], query_pos[None], key_pos.reshape(ctx_count, -1, 1), wout.reshape(width, width),
+        gu.reshape(2, width, -1), down_weight, dall, kv, qp,
+    )
+    kv_width = kv_weight.shape[1] // 2
+    q_raw = raw[:, :width].reshape(tokens, -1, head_size)
+    k_raw = raw[:, width:].reshape(tokens, -1, head_size)
+    q_scale, k_scale = root_scale(q_raw), root_scale(k_raw)
+    inputs = x.astype(f32)
+    scale_in = root_scale(inputs)
+    d_qnorm = unrotate(dq.reshape(q_raw.shape), cosine, sine_table)
+    d_knorm = unrotate(dkv[:, :kv_width].reshape(k_raw.shape), cosine, sine_table)
+    q_gain_grad = jnp.sum(d_qnorm * q_raw * q_scale, axis=(0, 1))
+    k_gain_grad = jnp.sum(d_knorm * k_raw * k_scale, axis=(0, 1))
+    d_qraw = norm_back(d_qnorm * q_gain, q_raw, q_scale).reshape(tokens, width).astype(bf16)
+    d_kraw = norm_back(d_knorm * k_gain, k_raw, k_scale).reshape(tokens, kv_width)
+    d_kvraw = jnp.concatenate([d_kraw, dkv[:, kv_width:]], axis=1).astype(bf16)
+    full = w.reshape(width, -1)
+    full_q, full_kv = full[:, :width], full[:, width:]
+    d_normed = back_dot(d_qraw, full_q) + back_dot(d_kvraw, full_kv)
+    in_gain_grad = jnp.sum(d_normed * inputs * scale_in, axis=0)
+    input_grad = (dy + norm_back(d_normed * norm_in, inputs, scale_in)).reshape(hidden_in.shape)
+    gain_list = (in_gain_grad, q_gain_grad, k_gain_grad, gmid[0])
+    packed = jnp.concatenate([term.reshape(ctx_count, -1) for term in gain_list], axis=1).reshape(-1)
+    grads = jnp.concatenate([outer_dot(h1, d_qraw), outer_dot(h1, d_kvraw), outer_dot(ob, dattn)], axis=1)
+
+    def summed(array):
+        share = lax.psum_scatter(array.astype(bf16), "ctx", scatter_dimension=0, tiled=True)
+        return lax.psum(share, "dp").astype(f32)
+
+    gains = summed(packed)
+    total_grads = summed(grads)
+    total_q, total_kv, total_out = (total_grads[:, i * width : (i + 1) * width] for i in range(3))
+    total_gate, total_up, total_down = (
+        lax.all_gather(piece, "dp", axis=1, tiled=True).astype(f32)
+        for piece in (gate_piece, up_piece, down_piece)
+    )
+    wide_piece = width // ctx_count
+    head_piece = head_size // ctx_count
+    return (
+        y.reshape(hidden_in.shape),
+        input_grad,
+        gains[:wide_piece],
+        total_q,
+        total_kv,
+        gains[wide_piece : wide_piece + head_piece],
+        gains[wide_piece + head_piece : wide_piece + 2 * head_piece],
+        total_out,
+        gains[wide_piece + 2 * head_piece :],
+        total_gate,
+        total_up,
+        total_down,
     )
 
 
@@ -355,8 +1347,9 @@
 
 
 def solution(mesh):
+    kernels = mesh.shape["dp"] == 4 and mesh.shape["ctx"] == 8
     return jax.shard_map(
-        per_device,
+        staged if kernels else per_device,
         mesh=mesh,
         in_specs=(
             P("dp", "ctx", None, None),

time: 1300 us -> 480 us (0.37)
  waiting for transfers between devices: 728 us -> 93.5 us
  Pallas kernels: 0 us -> 241 us
  matrix products: 217 us -> 7.62 us
  local copies, waits for them, and re-layouts: 168 us -> 55.1 us
  other arithmetic: 91.8 us -> 35.5 us
  loops' own time: 47.7 us -> 0 us
    reduce_scatter x8 -> x0, waiting for transfers between devices: 433 us -> none  [the longest x1 100 us: per_device(): lax.psum_scatter(gate_grad.astype(jnp.bfloat16), 'ctx', scatter_dimension...]
    pallas_call x0 -> x2, Pallas kernels: none -> 241 us  [the longest x1 140 us: middle(): pl.pallas_call(middle_kernel, out_shape=(shape((256, 1024), bf16), shape(...]
    all_gather x7 -> x3, waiting for transfers between devices: 223 us -> 7.94 us  [staged(): lax.all_gather(piece, 'dp', axis=1, tiled=True).astype(f32)]
    dot_general x62 -> x0, matrix products: 161 us -> none  [the longest x16 30.1 us: tile_of(): jnp.einsum('snqd,sknd->snqk', queries, key_tile, preferred_element_type=j...]
    dynamic_update_slice x16 -> x0, local copies, waits for them, and re-layouts: 53.8 us -> none  [the longest x8 26.9 us: grad_step(): lax.dynamic_update_slice_in_dim(d_values, value_part, tile_start, 1)]
    another operation x3 -> x0, loops' own time: 47.7 us -> none  [the longest x1 16 us: per_device(): lax.scan(grad_step, grad_state, tile_starts)]
    lt x24 -> x1, other arithmetic: 34 us -> 0.07 us  [staged(): valid = (query_pos < lengths[0])[:, None]]
    unnamed x16 -> x6, waiting for transfers between devices: 3.81 us -> 37.2 us
  transfers between devices with their start and end apart: 16 -> 5, of which waited for: 14 -> 3; matrix products, arithmetic and copies ran while one was open for 20% -> 4% of each run, Pallas kernels for 0% -> 0%
where the time goes in v1:
time: 480 us; the launch traced here: 474 us
  Pallas kernels  241 us (50%)
  waiting for transfers between devices  93.5 us (19%)
  local copies, waits for them, and re-layouts  55.1 us (11%)
  other arithmetic  35.5 us (7%)
  blocking collectives  23.6 us (5%)
  between operations  17.6 us (4%)
  matrix products  7.62 us (2%)
    pallas_call x1, Pallas kernels, middle(): pl.pallas_call(middle_kernel, out_shape=(shape((256, 1024), bf16), shape(...  140 us
    pallas_call x1, Pallas kernels, front(): pl.pallas_call(front_kernel, out_shape=(shape((256, 1024), bf16), shape((...  101 us
    psum x1, waiting for transfers between devices, summed(): return lax.psum(share, 'dp').astype(f32)  48.4 us
    unnamed x6, waiting for transfers between devices  37.2 us
    unnamed x54, local copies, waits for them, and re-layouts  16.8 us
    unnamed x1, blocking collectives  14.9 us
    concatenate x1, other arithmetic, staged(): jnp.concatenate([outer_dot(h1, d_qraw), outer_dot(h1, d_kvraw), outer_dot...  13.4 us
  transfers between devices with their start and end apart: 5, of which 3 were waited for; matrix products, arithmetic and copies ran while one was open for 4% of the time, Pallas kernels for 0%

profile of v1, /device:TPU:0, one launch (start us, length us, event | category | flops | bytes accessed | tf_op | source)
XLA Modules:
  0.0 474.1 jit_solution(8491900486974160667)
XLA Ops:
  8.1 0.7 dynamic-slice_multiply_fusion
  9.0 0.7 broadcast_multiply_fusion.3
  9.9 0.8 copy.82.sin_ref
  10.6 0.8 copy.81.cos_ref
  12.1 0.8 copy.83.qpos_ref
  13.0 0.7 tile.16
  13.6 0.6 broadcast_in_dim_tile.6.qg_ref
  14.2 0.7 tile.34
  14.9 0.6 broadcast_in_dim_tile.7.kg_ref
  15.6 1.9 bitcast_select_fusion.dffn_ref
  17.6 0.6 compare_select_fusion.1.kpos_ref
  18.2 100.8 %front.1 = (bf16[256,1024]{1,0:T(8,128)(2,1)}, f32[256,1536]{1,0:T(8,128)}, bf16[8,512,128]{2,1,0:T(8,128)(2,1)}, bf16[8,256,1024]{2,1,0:T(8,128)(2,1)}, bf16[25...) custom-call(bf16[256,1024]{1,0:T(8,128)(2,1)} %bitcast.70, ...), custom_call_target="tpu_custom_call" | custom-call | tf_op jit(solution)/shard_map/front/pallas_call | solution.py:576
  119.0 2.4 slice.52
  121.5 0.8 slice.56
  122.7 1.2 compare_select_fusion.kpos_ref
  123.9 139.9 %middle.1 = (bf16[256,1024]{1,0:T(8,128)(2,1)}, f32[256,1024]{1,0:T(8,128)}, bf16[256,1024]{1,0:T(8,128)(2,1)}, f32[1,1024]{1,0:T(1,128)}, f32[256,1024]{1,0:T(8...) custom-call(bf16[256,1024]{1,0:T(8,128)(2,1)} %bitcast.71, ...), custom_call_target="tpu_custom_call" | custom-call | tf_op jit(solution)/shard_map/middle/pallas_call | solution.py:935
  263.8 1.9 slice.57
  265.6 1.2 slice.98
  266.8 2.5 copy.86
  269.3 2.4 multiply_add_fusion
  271.7 1.3 copy.85
  273.0 1.9 multiply_reduce_fusion.2
  274.9 1.1 mul.333
  276.0 2.5 copy.88
  278.5 1.1 mul.348
  279.6 2.5 copy.89
  282.1 1.1 mul.354
  283.1 2.5 copy.90
  285.7 1.3 copy.87
  287.1 1.2 copy.92
  288.4 1.2 copy.91
  289.6 0.9 multiply_reduce_fusion.6
  290.6 1.0 copy.94
  291.6 1.0 copy.95
  292.7 1.0 copy.96
  293.7 2.1 copy.93
  295.9 2.1 convolution_convert_fusion
  298.0 0.6 multiply_reduce_fusion
  299.1 0.8 convolution_convert_fusion.2
  300.8 0.8 convolution_convert_fusion.1
  301.6 13.4 %pad_maximum_fusion = bf16[1024,3072]{0,1:T(8,128)(2,1)} fusion(bf16[1024,1024]{0,1:T(8,128)(2,1)S(1)} %convolution_convert_fusion, bf16[1024,1024]{0,1:T(8,128)(2,1)S(1)} %convolution_convert_fusion.1, bf16[1024,1024]{0,1:T(8,128)(2,1)S(1)} %convolution_convert_fusion.2), kind=kLoop, calls=%fused_computation | loop fusion | flops 18874368 | bytes 12582912 | tf_op jit(solution)/shard_map/concatenate | solution.py:1034
  314.9 8.6 %copy.104 = bf16[1024,3072]{1,0:T(8,128)(2,1)} copy(bf16[1024,3072]{0,1:T(8,128)(2,1)} %pad_maximum_fusion) | data formatting | bytes 12582912
  324.2 0.5 all-gather.6.cloned.1.call-update
  324.8 0.5 all-gather.8.cloned.1.call-update
  326.2 3.0 fusion
  329.5 1.0 fusion.12
  330.8 0.6 dynamic-slice
  332.0 14.9 %all-reduce = bf16[2176]{0:T(1024)(128)(2,1)S(1)} all-reduce(bf16[2176]{0:T(1024)(128)(2,1)S(1)} %convert_element_type.41), channel_id=2, replica_groups=mesh['dp'=4,'ctx'=8] {'ctx'}, use_global_device_ids=true, to_apply=%region_11.12.clone | all-reduce | flops 2176 | bytes 8704
  347.0 8.8 %psum.14 = bf16[272]{0:T(512)(128)(2,1)S(1)} all-reduce(bf16[272]{0:T(512)(128)(2,1)S(1)} %dynamic-slice.1), channel_id=1, replica_groups=mesh['dp'=4,'ctx'=8] {'dp'}, use_global_device_ids=true, to_apply=%region_12.13 | all-reduce | flops 272 | bytes 1088 | tf_op jit(solution)/shard_map/psum | solution.py:1038
  355.8 0.6 fusion.19
  356.3 35.6 %reduce-scatter.4.cloned.1.call-done = bf16[128,3072]{1,0:T(8,128)(2,1)} async-done(((bf16[1024,3072]{1,0:T(8,128)(2,1)}), bf16[128,3072]{1,0:T(8,128)(2,1)}) %reduce-scatter.4.cloned.1.call-update) | async-done | bytes 786448
  391.9 2.3 copy.105
  394.3 0.6 fusion.20
  394.9 1.3 fusion.9
  396.1 2.9 convert_element_type.44
  399.1 2.9 convert_element_type.45
  402.0 7.9 %all-gather.8.cloned.1.call-done = bf16[576,1024]{1,0:T(8,128)(2,1)} async-done(((bf16[576,256]{1,0:T(8,128)(2,1)}), bf16[576,1024]{1,0:T(8,128)(2,1)}) %all-gather.8.cloned.1.call-update) | async-done | bytes 1179664 | tf_op jit(solution)/shard_map/all_gather | solution.py:1044
  409.9 3.0 convert_element_type.46
  412.9 48.4 %all-reduce.3.cloned.1.call-done = bf16[128,3072]{0,1:T(8,128)(2,1)} async-done(((bf16[128,3072]{0,1:T(8,128)(2,1)}), bf16[128,3072]{0,1:T(8,128)(2,1)}) %all-reduce.3.cloned.1.call-update) | async-done | bytes 786448 | tf_op jit(solution)/shard_map/psum | solution.py:1038
  461.3 1.2 fusion.18
  462.5 1.0 copy.101
  463.5 1.0 copy.102
  464.5 1.0 copy.103
  465.5 0.8 copy.110
  (96 shorter events, 5.0 us)
Async XLA Ops:
  8.0 383.9 %reduce-scatter.4.cloned.1.call-start = ((), (), s32[]{:S(2)}) async-start(), calls=%async_computation.5 | async-start | bytes 7077888
  9.0 110.0 %copy-start.17 = (s32[2,128]{1,0:T(2,128)}, s32[2,128]{1,0:T(2,128)S(1)}, u32[]{:S(2)}) copy-start(s32[2,128]{1,0:T(2,128)S(1)} %iota_add_fusion) | copy-start | bytes 3076
  119.0 2.4 copy-start.1
  265.6 6.1 %copy-start.2 = (f32[256,1024]{1,0:T(8,128)S(1)}, f32[256,1024]{1,0:T(8,128)}, u32[]{:S(2)}) copy-start(f32[256,1024]{1,0:T(8,128)} %slice.52) | copy-start | bytes 3145732
  269.3 3.7 copy-start.20
  285.7 4.0 copy-start.19
  293.7 4.3 copy-start.3
  295.9 2.1 copy-start.4
  295.9 2.1 copy-start.5
  295.9 2.2 copy-start.6
  298.0 1.0 copy-start.7
  298.7 2.1 copy-start.12
  298.7 1.3 copy-start.8
  298.7 1.4 copy-start.9
  298.7 1.6 copy-start.10
  298.7 1.7 copy-start.11
  323.5 2.4 copy-start.18
  323.5 2.4 copy-start
  323.6 72.6 %all-gather.4.cloned.1.call-start = ((), (), s32[]{:S(2)}) async-start(), calls=%async_computation.2 | async-start | bytes 1474560 | tf_op jit(solution)/shard_map/all_gather | solution.py:1044
  324.1 74.9 %all-gather.6.cloned.1.call-start = ((), (), s32[]{:S(2)}) async-start(), calls=%async_computation.3 | async-start | bytes 1474560 | tf_op jit(solution)/shard_map/all_gather | solution.py:1044
  324.7 85.2 %all-gather.8.cloned.1.call-start = ((), (), s32[]{:S(2)}) async-start(), calls=%async_computation.4 | async-start | bytes 1474560 | tf_op jit(solution)/shard_map/all_gather | solution.py:1044
  325.3 135.9 %all-reduce.3.cloned.1.call-start = ((), (), s32[]{:S(2)}) async-start(), calls=%async_computation.1 | async-start | bytes 1572864 | tf_op jit(solution)/shard_map/psum | solution.py:1038
  326.0 3.4 copy-start.21
  326.2 3.4 copy-start.13
  326.2 3.4 copy-start.16
  329.5 1.2 copy-start.22
  330.6 64.3 %copy-start.14 = (f32[256,1024]{1,0:T(8,128)S(1)}, f32[256,1024]{1,0:T(8,128)}, u32[]{:S(2)}) copy-start(f32[256,1024]{1,0:T(8,128)} %get-tuple-element.41) | copy-start | bytes 3145732
  462.5 3.0 copy-start.15
Sparse Core Ops, SparseCore 0:
  323.7 68.1 reduce-scatter.3
Sparse Core Ops, SparseCore 1:
  325.9 25.3 all-gather.3
  352.9 27.8 all-gather.5
  382.5 27.4 all-gather.7
  413.0 48.2 all-reduce.2

commit v2 on v1

--- a/solution.py
+++ b/solution.py
@@ -274,7 +274,7 @@
 def front_kernel(
     x_ref, norm_ref, qw_ref, kvw_ref, outw_ref, gate_ref, up_ref, dffn_ref, cos_ref, sin_ref, qg_ref,
     kg_ref, qpos_ref, kpos_ref,
-    h1_ref, raw_ref, qp_ref, kv_ref, ob_ref, o_ref, lrow_ref, w_ref, wout_ref, gu_ref, dall_ref,
+    h1_ref, raw_ref, qp_ref, kv_ref, ob_ref, lrow_ref, w_ref, wout_ref, gu_ref, dall_ref,
     acc_ref, sum_ref, bias_ref,
     loc, wsend, wrecv, osend, orecv, dsend, drecv, gsend, grecv, lsend, lrecv, ssend, srecv,
 ):
@@ -504,7 +504,6 @@
             chunk = jnp.where(low, even, pltpu.roll(odd, 64, 1))
         else:
             chunk = jnp.where(low, pltpu.roll(even, 64, 1), odd)
-        o_ref[:, 128 * n : 128 * (n + 1)] = chunk
         ob_ref[:, 128 * n : 128 * (n + 1)] = chunk.astype(bf16)
         whole = jnp.where(low, weight[0:256], weight[256:512])
         rows = exact_nt(head_marks(n), jnp.log2(whole)) * (1.0 / 64)
@@ -581,7 +580,6 @@
             shape((8, 512, 128), bf16),
             shape((8, 256, 1024), bf16),
             shape((256, 1024), bf16),
-            shape((256, 1024), f32),
             shape((16, 256), f32),
             shape((4, 256, 2048), bf16),
             shape((4, 256, 1024), bf16),
@@ -589,7 +587,7 @@
             shape((4, 256, 1024), bf16),
         ),
         in_specs=[vmem(), vmem()] + [anywhere()] * 6 + [vmem()] * 6,
-        out_specs=[vmem()] * 11,
+        out_specs=[vmem()] * 10,
         scratch_shapes=[
             pltpu.VMEM((256, 2048), f32),
             pltpu.VMEM((8, 512, 256), f32),
@@ -683,25 +681,70 @@
         self.far_copy().wait_send()
 
 
-def middle_kernel(
-    x_ref, ob_ref, o_ref, lrow_ref, nmid_ref, qpos_ref, kpos_ref, wout_ref, gu_hbm, down_hbm, dall_hbm, kv_hbm, qp_hbm,
-    y_ref, dy_ref, dattn_ref, gmid_ref, dq_ref, dkv_ref, gate_ref, up_ref, downg_ref,
-    gu, down, dall, kv, qp, h2, act, y1, own_y, own_p, y_out, p_out, y_in, p_in,
+class Spread:
+    def __init__(self, source, target, send, recv):
+        self.source, self.target, self.send, self.recv = source, target, send, recv
+        self.d, self.ctx, self.z, self.c = place_of()
+
+    def columns(self, j):
+        return pl.ds(pl.multiple_of(256 * flip(self.d, j), 256), 256)
+
+    def copy(self, j):
+        return remote(
+            self.source.at[:, self.columns(j)],
+            self.target.at[j],
+            self.send.at[j],
+            self.recv.at[j],
+            (flip(self.d, j), self.ctx),
+        )
+
+    def start(self):
+        for j in (3, 1, 2):
+            self.copy(j).start()
+        self.target[0] = self.source[:, self.columns(0)]
+
+    def landed(self):
+        for j in NEIGHBOURS:
+            self.copy(j).wait_recv()
+
+    def drain(self):
+        for j in NEIGHBOURS:
+            self.copy(j).wait_send()
+
+
+def local_copy(source, target, sem):
+    copy = pltpu.make_async_copy(source, target, sem)
+    copy.start()
+    copy.wait()
+
+
+def back_kernel(
+    x_ref, ob_ref, lrow_ref, nmid_ref, nin_ref, qpos_ref, kpos_ref, wout_ref, raw_ref, cos_ref, sin_ref, qg_ref, kg_ref,
+    gu_hbm, down_hbm, dall_hbm, kv_hbm, qp_hbm, h1_hbm, w_hbm,
+    y_ref, ig_ref, gains_ref, gate_all, up_all, down_all, qkvo_all,
+    gu, down, dall, kv, qp, h2, act, y1, own_p, y_out, p_out, y_in, p_in,
     dop, dqt, bias, core_in, near_in, far_in, dcore, dsum, dnear, dfar, kcore, knear, kfar,
+    h1_all, ob_all, cols_in, wcore, wnear, wfar, piece, dpiece, gsum, gin,
     loc, hsend, hrecv, psend, precv, ysend, yrecv, gsend, grecv, usend, urecv, dsend, drecv, asend, arecv, ksend, krecv,
+    h1send, h1recv, obsend, obrecv, csend, crecv, wsend, wrecv, agsend, agrecv, ausend, aurecv, adsend, adrecv,
+    aqsend, aqrecv, nsend, nrecv,
 ):
     d, ctx, z, c = place_of()
     sibling = (d, 2 * z + 1 - c)
-    width = act.shape[2]
     barrier, count = greet((1, 2, 3), True, "pair", True)
+    cut_width = act.shape[2] // 3
+    cuts = [slice(i * cut_width, (i + 1) * cut_width) for i in range(3)]
     loads = [
         pltpu.make_async_copy(source, target, loc.at[slot])
         for slot, (source, target) in enumerate(
-            ((gu_hbm, gu), (down_hbm, down), (dall_hbm, dall), (kv_hbm, kv), (qp_hbm, qp))
+            (
+                (gu_hbm, gu), (down_hbm, down), (dall_hbm, dall), (kv_hbm, kv), (qp_hbm, qp), (h1_hbm, h1_all.at[0]),
+            )
         )
     ]
     for copy in loads:
         copy.start()
+    ob_all[0] = ob_ref[...]
 
     residual = x_ref[...].astype(f32) + nn(ob_ref[...], wout_ref[...])
     y1[...] = residual
@@ -717,55 +760,45 @@
         rows = 256 * blocks
         span = slice(first * 256, first * 256 + rows)
         tokens = h2[first : first + blocks].reshape(rows, 1024)
-        grads = dall[first : first + blocks].reshape(rows, 1024)
-        gate = nn(tokens, gu[0])
-        up = nn(tokens, gu[1])
-        sig = jax.nn.sigmoid(gate)
-        silu = gate * sig
-        act[0, span, :] = (silu * up).astype(bf16)
-        dact = nt(grads, down[...])
-        act[1, span, :] = (dact * up * sig * (1.0 + gate * (1.0 - sig))).astype(bf16)
-        act[2, span, :] = (dact * silu).astype(bf16)
+        cot = dall[first : first + blocks].reshape(rows, 1024)
+        for cut in cuts:
+            gate = nn(tokens, gu[0, :, cut])
+            up = nn(tokens, gu[1, :, cut])
+            sig = jax.nn.sigmoid(gate)
+            silu = gate * sig
+            act[0, span, cut] = (silu * up).astype(bf16)
+            dact = nt(cot, down[cut, :])
+            act[1, span, cut] = (dact * up * sig * (1.0 + gate * (1.0 - sig))).astype(bf16)
+            act[2, span, cut] = (dact * silu).astype(bf16)
         part = nt(act[1, span, :], gu[0]) + nt(act[2, span, :], gu[1])
         if first == 0:
             own_p[...] = part
         else:
             p_out[first - 1 : first - 1 + blocks] = part.astype(bf16).reshape(blocks, 256, 1024)
-        return span
 
     def ffn_out(first, blocks):
-        span = slice(first * 256, first * 256 + 256 * blocks)
-        part = nn(act[0, span, :], down[...])
-        if first == 0:
-            own_y[...] = part
-        else:
-            y_out[first - 1 : first - 1 + blocks] = part.astype(bf16).reshape(blocks, 256, 1024)
-
-    def scatter(out_buf, in_buf, send, recv, k):
-        return remote(out_buf.at[k - 1], in_buf.at[k - 1], send.at[k - 1], recv.at[k - 1], (flip(d, k), ctx))
+        part = nn(act[0, first * 256 : (first + blocks) * 256, :], down[...])
+        y_out[first : first + blocks] = part.astype(bf16).reshape(blocks, 256, 1024)
+
+    def scatter_p(k):
+        return remote(p_out.at[k - 1], p_in.at[k - 1], psend.at[k - 1], precv.at[k - 1], (flip(d, k), ctx))
+
+    def scatter_y(k):
+        return remote(y_out.at[k], y_in.at[k - 1], ysend.at[k - 1], yrecv.at[k - 1], (flip(d, k), ctx))
 
     ffn(0, 1)
     gather.hop_near()
     ffn(1, 2)
-    scatter(p_out, p_in, psend, precv, 1).start()
-    scatter(p_out, p_in, psend, precv, 2).start()
+    scatter_p(1).start()
+    scatter_p(2).start()
     gather.hop_far()
     ffn(3, 1)
-    scatter(p_out, p_in, psend, precv, 3).start()
+    scatter_p(3).start()
     ffn_out(0, 1)
     ffn_out(1, 2)
     ffn_out(3, 1)
-    for k in NEIGHBOURS:
-        scatter(y_out, y_in, ysend, yrecv, k).start()
 
     tokens = h2[...].reshape(1024, 1024)
-    down[...] = tn(act[0], dall[...].reshape(1024, 1024)).astype(bf16)
-    half = down.shape[0] // 2
-
-    def down_core():
-        return remote(down.at[pl.ds(half * (1 - c), half)], dcore, dsend.at[0], drecv.at[0], sibling)
-
-    down_core().start()
     gu[0] = tn(tokens, act[1]).astype(bf16)
 
     def weight_sum(t, send, recv):
@@ -785,50 +818,70 @@
     gu[1] = tn(tokens, act[2]).astype(bf16)
     for r in (3, 1, 2, 0):
         up_sum.begin(r)
-
-    down_core().wait_recv()
+    down[...] = tn(act[0], dall[...].reshape(1024, 1024)).astype(bf16)
+    half = down.shape[0] // 2
+
+    def down_core():
+        return remote(down.at[pl.ds(half * (1 - c), half)], dcore, dsend.at[0], drecv.at[0], sibling)
 
     def down_piece(j):
         return down.at[pl.ds(half * c, half), pl.ds(pl.multiple_of(256 * flip(d, j), 256), 256)]
 
-    down_mine = down.at[pl.ds(half * c, half)]
-    down_mine[...] = total(down_mine, dcore).astype(bf16)
-
     def down_copy(j):
         return remote(down_piece(j), dsum.at[d], dsend.at[j], drecv.at[j], (flip(d, j), ctx))
 
     def down_landed(j):
-        piece = dsum.at[flip(d, j)]
-        remote(piece, piece, dsend.at[j], drecv.at[j], (flip(d, j), ctx)).wait_recv()
-
-    for j in NEIGHBOURS:
-        down_copy(j).start()
-    dsum[d] = down_piece(0)[...]
-
-    def part_sum(item, rs):
-        for r in rs:
+        block = dsum.at[flip(d, j)]
+        remote(block, block, dsend.at[j], drecv.at[j], (flip(d, j), ctx)).wait_recv()
+
+    down_core().start()
+
+    def part_sum(item):
+        for r in (3, 1, 2, 0):
             item.add_core(r)
             if r in (1, 3):
                 item.pass_near(r)
 
-    part_sum(gate_sum, (3, 1, 2, 0))
-    part_sum(up_sum, (3, 1, 2, 0))
+    part_sum(gate_sum)
+    part_sum(up_sum)
+    down_core().wait_recv()
+    down_mine = down.at[pl.ds(half * c, half)]
+    down_mine[...] = total(down_mine, dcore).astype(bf16)
 
     dmid = own_p[...]
     for k in NEIGHBOURS:
-        scatter(p_out, p_in, psend, precv, k).wait_recv()
+        scatter_p(k).wait_recv()
         dmid = dmid + p_in[k - 1].astype(f32)
+    for k in NEIGHBOURS:
+        scatter_p(k).wait_send()
+    gather.drain()
+    rows_in = p_out
+
+    for j in (3, 1, 2):
+        down_copy(j).start()
+    dsum[d] = down_piece(0)[...]
+    loads[5].wait()
+    ob_gather = Gather(ob_all, obsend, obrecv, 0, 256, "relative")
+    h1_gather = Gather(h1_all, h1send, h1recv, 0, 256, "relative")
+
     residual = y1[...]
     scale = lax.rsqrt(jnp.mean(residual * residual, axis=-1, keepdims=True) + epsilon)
-    gmid_ref[...] = jnp.sum(dmid * residual * scale, axis=0, keepdims=True)
+    gmid = jnp.sum(dmid * residual * scale, axis=0, keepdims=True)
+    for i in range(8):
+        gsum[i : i + 1, :] = gmid[:, 128 * i : 128 * (i + 1)]
     scaled = dmid * nmid_ref[...]
     dy = dall[0].astype(f32) + scale * scaled - residual * (scale * scale * scale) * jnp.mean(
         scaled * residual, axis=-1, keepdims=True
     )
-    dy_ref[...] = dy
-    dattn = dy.astype(bf16)
-    dattn_ref[...] = dattn
-    d_mixed = nt(dattn, wout_ref[...])
+    own_p[...] = dy
+    rows_in[0] = dy.astype(bf16)
+
+    def spread(i):
+        return Spread(rows_in.at[i], cols_in.at[i], csend.at[i], crecv.at[i])
+
+    ob_gather.start()
+    spread(0).start()
+    d_mixed = nt(rows_in[0], wout_ref[...])
     low = lanes(256) < 64
     delta = None
     for n in range(8):
@@ -840,7 +893,7 @@
             even, odd = jnp.where(low, 0.0, other), jnp.where(low, 0.0, u)
         dop[n, 0:256] = even.astype(bf16)
         dop[n, 256:512] = odd.astype(bf16)
-        rows = exact_nt(head_marks(n), u * o_ref[:, 128 * n : 128 * (n + 1)])
+        rows = exact_nt(head_marks(n), u * ob_ref[:, 128 * n : 128 * (n + 1)].astype(f32))
         delta = rows if delta is None else delta + rows
 
     loads[3].wait()
@@ -860,21 +913,51 @@
     lrow = lrow_ref[...]
 
     def attend_back(block, target):
-        bias[...] = jnp.where(kpos_ref[block] <= qpos_ref[...], 0.0, masked_score)
+        places = jnp.broadcast_to(kpos_ref[block].astype(f32), (256, 256)).T
+        bias[...] = jnp.where(places <= qpos_ref[...].astype(f32), 0.0, masked_score)
         for m in range(4):
             keys = kv[block, :, 128 * m : 128 * (m + 1)]
             values = kv[block, :, 512 + 128 * m : 512 + 128 * (m + 1)]
             queries = qp[2 * m : 2 * m + 2].reshape(1024, 128)
-            grads = dop[2 * m : 2 * m + 2].reshape(1024, 128)
+            cot = dop[2 * m : 2 * m + 2].reshape(1024, 128)
             scores = nt(keys, queries) * to_exponent - row_of(lrow, m)
             weights = jnp.concatenate(
                 [jnp.exp2(scores[:, 256 * i : 256 * (i + 1)] + bias[...]) for i in range(4)], axis=1
             )
-            dweights = nt(values, grads)
+            dweights = nt(values, cot)
             dscores = (weights * (dweights - row_of(delta, m))).astype(bf16)
             target[:, 128 * m : 128 * (m + 1)] = (nn(dscores, queries) * 0.125).astype(bf16)
-            target[:, 512 + 128 * m : 512 + 128 * (m + 1)] = nn(weights.astype(bf16), grads).astype(bf16)
+            target[:, 512 + 128 * m : 512 + 128 * (m + 1)] = nn(weights.astype(bf16), cot).astype(bf16)
             dqt[m] += tn(keys, dscores)
+
+    down_sum = CtxSum(lambda r, core: dsum.at[flip(z, r)], None, dnear, dfar, asend, arecv)
+
+    def grad_sum(i):
+        return CtxSum(
+            lambda r, core: h2.at[flip(z, r), pl.ds(128 * core, 128), pl.ds(256 * i, 256)],
+            wcore.at[i],
+            wnear.at[i],
+            wfar.at[i],
+            wsend.at[i],
+            wrecv.at[i],
+        )
+
+    def grad_begin(i, tokens_all):
+        spread(i).landed()
+        grad = tn(tokens_all[...].reshape(1024, 1024), cols_in[i].reshape(1024, 256)).astype(bf16)
+        h2[:, :, 256 * i : 256 * (i + 1)] = grad.reshape(4, 256, 256)
+        for r in (3, 1, 2, 0):
+            grad_sum(i).begin(r)
+
+    gate_gather = Gather(gate_all, agsend, agrecv, 0, 128, "absolute")
+    up_gather = Gather(up_all, ausend, aurecv, 0, 128, "absolute")
+    down_gather = Gather(down_all, adsend, adrecv, 0, half, "absolute")
+    qkvo_gather = Gather(qkvo_all, aqsend, aqrecv, 0, 128, "absolute")
+
+    def publish(item, stage, target, slot, gathering):
+        stage[...] = item.result().astype(bf16)
+        local_copy(stage, target.at[d], loc.at[slot])
+        gathering.start()
 
     for r in (3, 1, 2, 0):
         for core in (0, 1):
@@ -885,17 +968,34 @@
             dkv_sum.pass_near(r)
         if r == 3:
             gate_sum.pass_far()
+            ob_gather.hop_near()
+            h1_gather.start()
         if r == 1:
             up_sum.pass_far()
-        if r == 2:
             for j in NEIGHBOURS:
                 down_landed(j)
-
-    down_sum = CtxSum(
-        lambda r, core: dsum.at[flip(z, r)], None, dnear, dfar, asend, arecv
-    )
-    down_sum.pass_near(3)
-    down_sum.pass_near(1)
+            down_sum.pass_near(3)
+            down_sum.pass_near(1)
+            ob_gather.hop_far()
+            h1_gather.hop_near()
+            for k in NEIGHBOURS:
+                scatter_y(k).start()
+        if r == 2:
+            grad_begin(0, ob_all)
+            h1_gather.hop_far()
+
+    cosine, sine = cos_ref[...], sin_ref[...]
+
+    def unturn(u):
+        return u * cosine - half_turn(u) * sine
+
+    def norm_unwind(grad, value, gain):
+        scale = lax.rsqrt(head_sum(value * value) * (1.0 / 64) + epsilon)
+        moved = grad * gain
+        back = scale * moved - value * (scale * scale * scale) * (head_sum(moved * value) * (1.0 / 64))
+        return back, jnp.sum(grad * value * scale, axis=0, keepdims=True)
+
+    qgain = None
     for n in range(8):
         m, e = n // 2, n % 2
         turned = dqt[m, :, 512 * e : 512 * (e + 1)].T
@@ -904,49 +1004,121 @@
             chunk = jnp.where(low, even, pltpu.roll(odd, 64, 1))
         else:
             chunk = jnp.where(low, pltpu.roll(even, 64, 1), odd)
-        dq_ref[:, 128 * n : 128 * (n + 1)] = chunk * 0.125
+        back, gain = norm_unwind(unturn(chunk * 0.125), raw_ref[:, 128 * n : 128 * (n + 1)], qg_ref[...])
+        rows_in[1, :, 128 * n : 128 * (n + 1)] = back.astype(bf16)
+        qgain = gain if qgain is None else qgain + gain
+    gsum[16:17, :] = qgain
+    spread(1).start()
+    weights = [
+        pltpu.make_async_copy(w_hbm.at[:, :, pl.ds(1024 * i, 1024)], kv.at[pl.ds(4 * i, 4)], loc.at[6 + 5 * i])
+        for i in (0, 1)
+    ]
+    for copy in weights:
+        copy.start()
+
     dkv_sum.pass_far()
     down_sum.pass_far()
-    gate_ref[...] = gate_sum.result().astype(bf16)
-    up_ref[...] = up_sum.result().astype(bf16)
-    out = y1[...] + own_y[...]
+    publish(gate_sum, piece.at[0], gate_all, 7, gate_gather)
+    grad_begin(1, h1_all)
+    part_sum(grad_sum(0))
+    publish(up_sum, piece.at[1], up_all, 8, up_gather)
+    for copy in weights:
+        copy.wait()
+    dh1 = nt(rows_in[1], kv[0:4].reshape(1024, 1024))
+    gate_gather.hop_near()
+    out = y1[...] + y_out[0].astype(f32)
     for k in NEIGHBOURS:
-        scatter(y_out, y_in, ysend, yrecv, k).wait_recv()
+        scatter_y(k).wait_recv()
         out = out + y_in[k - 1].astype(f32)
     y_ref[...] = out.astype(bf16)
-    dkv_ref[...] = dkv_sum.result()
-    downg_ref[...] = down_sum.result().astype(bf16)
-
-    gather.drain()
+    part_sum(grad_sum(1))
+
+    dkv = dkv_sum.result()
+    kgain = None
+    for n in range(4):
+        span = slice(128 * n, 128 * (n + 1))
+        back, gain = norm_unwind(unturn(dkv[:, span]), raw_ref[:, 1024 + 128 * n : 1152 + 128 * n], kg_ref[...])
+        rows_in[2, :, span] = back.astype(bf16)
+        kgain = gain if kgain is None else kgain + gain
+    rows_in[2, :, 512:] = dkv[:, 512:].astype(bf16)
+    gsum[17:18, :] = kgain
+    spread(2).start()
+    dh1 = dh1 + nt(rows_in[2], kv[4:8].reshape(1024, 1024))
+    x = x_ref[...].astype(f32)
+    scale = lax.rsqrt(jnp.mean(x * x, axis=-1, keepdims=True) + epsilon)
+    gin_grad = jnp.sum(dh1 * x * scale, axis=0, keepdims=True)
+    for i in range(8):
+        gsum[8 + i : 9 + i, :] = gin_grad[:, 128 * i : 128 * (i + 1)]
+    gsum[18:24, :] = jnp.zeros((6, 128), f32)
+
+    def gain_copy(slot, device):
+        return remote(gsum, gin.at[slot], nsend.at[slot], nrecv.at[slot], device)
+
+    gain_copy(0, sibling).start()
+    scaled = dh1 * nin_ref[...]
+    ig_ref[...] = own_p[...] + scale * scaled - x * (scale * scale * scale) * jnp.mean(
+        scaled * x, axis=-1, keepdims=True
+    )
+    grad_begin(2, h1_all)
+    gain_copy(0, sibling).wait()
+    gsum[...] = gsum[...] + gin[0]
     for k in NEIGHBOURS:
-        scatter(p_out, p_in, psend, precv, k).wait_send()
-        scatter(y_out, y_in, ysend, yrecv, k).wait_send()
+        gain_copy(k, (flip(d, k), ctx)).start()
+    part_sum(grad_sum(2))
+    grad_sum(0).pass_far()
+    grad_sum(1).pass_far()
+    up_gather.hop_near()
+    gate_gather.hop_far()
+    publish(down_sum, dpiece, down_all, 9, down_gather)
+    for k in NEIGHBOURS:
+        gain_copy(k, (flip(d, k), ctx)).wait()
+    gsum[...] = gsum[...] + gin[1] + gin[2] + gin[3]
+    gain_copy(4, (d, 2 * flip(z, 1) + c)).start()
+    grad_sum(2).pass_far()
+    up_gather.hop_far()
+    gain_copy(4, (d, 2 * flip(z, 1) + c)).wait()
+    gsum[...] = gsum[...] + gin[4]
+    gain_copy(5, (d, 2 * flip(z, 2) + c)).start()
+    down_gather.hop_near()
+    for i, at in ((0, 512), (1, 0), (2, 256)):
+        piece[0, :, at : at + 256] = grad_sum(i).result().astype(bf16)
+    local_copy(piece.at[0, :, pl.ds(0, 768)], qkvo_all.at[d], loc.at[10])
+    qkvo_gather.start()
+    gain_copy(5, (d, 2 * flip(z, 2) + c)).wait()
+    gains_ref[...] = gsum[...] + gin[5]
+    down_gather.hop_far()
+    qkvo_gather.hop_near()
+    qkvo_gather.hop_far()
+
+    for gathering in (ob_gather, h1_gather, gate_gather, up_gather, down_gather, qkvo_gather):
+        gathering.drain()
+    for k in NEIGHBOURS:
+        scatter_y(k).wait_send()
         down_copy(k).wait_send()
     down_core().wait_send()
-    gate_sum.drain()
-    up_sum.drain()
+    for item in (gate_sum, up_sum, dkv_sum, grad_sum(0), grad_sum(1), grad_sum(2)):
+        item.drain()
     down_sum.drain(core=False)
-    dkv_sum.drain()
-
-
-def middle(x, ob, o, lrow, norm_mid, qpos, kpos, wout, gu, down, dall, kv, qp):
+    for i in range(3):
+        spread(i).drain()
+
+
+def back(x, ob, lrow, norm_mid, norm_in, qpos, kpos, wout, raw, cosine, sine, q_gain, k_gain, gu, down, dall, kv, qp, h1, w):
     width = gu.shape[2]
     half = width // 2
     return pl.pallas_call(
-        middle_kernel,
+        back_kernel,
         out_shape=(
             shape((256, 1024), bf16),
             shape((256, 1024), f32),
-            shape((256, 1024), bf16),
-            shape((1, 1024), f32),
-            shape((256, 1024), f32),
-            shape((256, 1024), f32),
-            shape((128, width), bf16),
-            shape((128, width), bf16),
-            shape((half, 256), bf16),
+            shape((24, 128), f32),
+            shape((4, 128, width), bf16),
+            shape((4, 128, width), bf16),
+            shape((4, half, 256), bf16),
+            shape((4, 128, 768), bf16),
         ),
-        in_specs=[vmem()] * 8 + [anywhere()] * 5,
-        out_specs=[vmem()] * 9,
+        in_specs=[vmem()] * 13 + [anywhere()] * 7,
+        out_specs=[vmem()] * 3 + [anywhere()] * 4,
         scratch_shapes=[
             pltpu.VMEM((2, 1024, width), bf16),
             pltpu.VMEM((width, 1024), bf16),
@@ -957,8 +1129,7 @@
             pltpu.VMEM((3, 1024, width), bf16),
             pltpu.VMEM((256, 1024), f32),
             pltpu.VMEM((256, 1024), f32),
-            pltpu.VMEM((256, 1024), f32),
-            pltpu.VMEM((3, 256, 1024), bf16),
+            pltpu.VMEM((4, 256, 1024), bf16),
             pltpu.VMEM((3, 256, 1024), bf16),
             pltpu.VMEM((3, 256, 1024), bf16),
             pltpu.VMEM((3, 256, 1024), bf16),
@@ -975,12 +1146,25 @@
             pltpu.VMEM((4, 256, 1024), bf16),
             pltpu.VMEM((2, 256, 1024), bf16),
             pltpu.VMEM((256, 1024), bf16),
-            sems(5), sems(4), sems(4), sems(3), sems(3), sems(3), sems(3), sems(7), sems(7), sems(7), sems(7),
-            sems(4), sems(4), sems(7), sems(7), sems(7), sems(7),
+            pltpu.VMEM((4, 256, 1024), bf16),
+            pltpu.VMEM((4, 256, 1024), bf16),
+            pltpu.VMEM((3, 4, 256, 256), bf16),
+            pltpu.VMEM((3, 4, 128, 256), bf16),
+            pltpu.VMEM((3, 2, 128, 256), bf16),
+            pltpu.VMEM((3, 128, 256), bf16),
+            pltpu.VMEM((2, 128, width), bf16),
+            pltpu.VMEM((half, 256), bf16),
+            pltpu.VMEM((24, 128), f32),
+            pltpu.VMEM((6, 24, 128), f32),
+            sems(12), sems(4), sems(4), sems(3), sems(3), sems(3), sems(3), sems(7), sems(7), sems(7), sems(7),
+            sems(4), sems(4), sems(7), sems(7), sems(7), sems(7), sems(4), sems(4), sems(4), sems(4),
+            pltpu.SemaphoreType.DMA((3, 4)), pltpu.SemaphoreType.DMA((3, 4)),
+            pltpu.SemaphoreType.DMA((3, 7)), pltpu.SemaphoreType.DMA((3, 7)),
+            sems(4), sems(4), sems(4), sems(4), sems(4), sems(4), sems(4), sems(4), sems(6), sems(6),
         ],
-        compiler_params=pltpu.CompilerParams(collective_id=2, has_side_effects=True, vmem_limit_bytes=62 * 2**20),
-        name="middle",
-    )(x, ob, o, lrow, norm_mid, qpos, kpos, wout, gu, down, dall, kv, qp)
+        compiler_params=pltpu.CompilerParams(collective_id=2, has_side_effects=True, vmem_limit_bytes=63 * 2**20),
+        name="back",
+    )(x, ob, lrow, norm_mid, norm_in, qpos, kpos, wout, raw, cosine, sine, q_gain, k_gain, gu, down, dall, kv, qp, h1, w)
 
 
 def staged(
@@ -1003,62 +1187,39 @@
     x = hidden_in.reshape(tokens, width)
     valid = (query_pos < lengths[0])[:, None]
     dffn = jnp.where(valid, cotangent.reshape(tokens, width), jnp.zeros((), bf16))
-    h1, raw, qp, kv, ob, o, lrow, w, wout, gu, dall = front(
+    gains_wide = (jnp.tile(q_gain, 2)[None], jnp.tile(k_gain, 2)[None])
+    h1, raw, qp, kv, ob, lrow, w, wout, gu, dall = front(
         x, norm_in[None], q_weight, kv_weight, out_weight, gate_weight, up_weight, dffn, cos_wide, sin_wide,
-        jnp.tile(q_gain, 2)[None], jnp.tile(k_gain, 2)[None], query_pos[:, None], key_pos.reshape(ctx_count, 1, -1),
-    )
-    y, dy, dattn, gmid, dq, dkv, gate_piece, up_piece, down_piece = middle(
-        x, ob, o, lrow, norm_mid[None], query_pos[None], key_pos.reshape(ctx_count, -1, 1), wout.reshape(width, width),
-        gu.reshape(2, width, -1), down_weight, dall, kv, qp,
-    )
-    kv_width = kv_weight.shape[1] // 2
-    q_raw = raw[:, :width].reshape(tokens, -1, head_size)
-    k_raw = raw[:, width:].reshape(tokens, -1, head_size)
-    q_scale, k_scale = root_scale(q_raw), root_scale(k_raw)
-    inputs = x.astype(f32)
-    scale_in = root_scale(inputs)
-    d_qnorm = unrotate(dq.reshape(q_raw.shape), cosine, sine_table)
-    d_knorm = unrotate(dkv[:, :kv_width].reshape(k_raw.shape), cosine, sine_table)
-    q_gain_grad = jnp.sum(d_qnorm * q_raw * q_scale, axis=(0, 1))
-    k_gain_grad = jnp.sum(d_knorm * k_raw * k_scale, axis=(0, 1))
-    d_qraw = norm_back(d_qnorm * q_gain, q_raw, q_scale).reshape(tokens, width).astype(bf16)
-    d_kraw = norm_back(d_knorm * k_gain, k_raw, k_scale).reshape(tokens, kv_width)
-    d_kvraw = jnp.concatenate([d_kraw, dkv[:, kv_width:]], axis=1).astype(bf16)
-    full = w.reshape(width, -1)
-    full_q, full_kv = full[:, :width], full[:, width:]
-    d_normed = back_dot(d_qraw, full_q) + back_dot(d_kvraw, full_kv)
-    in_gain_grad = jnp.sum(d_normed * inputs * scale_in, axis=0)
-    input_grad = (dy + norm_back(d_normed * norm_in, inputs, scale_in)).reshape(hidden_in.shape)
-    gain_list = (in_gain_grad, q_gain_grad, k_gain_grad, gmid[0])
-    packed = jnp.concatenate([term.reshape(ctx_count, -1) for term in gain_list], axis=1).reshape(-1)
-    grads = jnp.concatenate([outer_dot(h1, d_qraw), outer_dot(h1, d_kvraw), outer_dot(ob, dattn)], axis=1)
-
-    def summed(array):
-        share = lax.psum_scatter(array.astype(bf16), "ctx", scatter_dimension=0, tiled=True)
-        return lax.psum(share, "dp").astype(f32)
-
-    gains = summed(packed)
-    total_grads = summed(grads)
-    total_q, total_kv, total_out = (total_grads[:, i * width : (i + 1) * width] for i in range(3))
-    total_gate, total_up, total_down = (
-        lax.all_gather(piece, "dp", axis=1, tiled=True).astype(f32)
-        for piece in (gate_piece, up_piece, down_piece)
-    )
-    wide_piece = width // ctx_count
-    head_piece = head_size // ctx_count
+        *gains_wide, query_pos[:, None], key_pos.reshape(ctx_count, 1, -1),
+    )
+    y, input_grad, sums, gate_all, up_all, down_all, qkvo_all = back(
+        x, ob, lrow, norm_mid[None], norm_in[None], query_pos[None], key_pos.reshape(ctx_count, 1, -1),
+        wout.reshape(width, width), raw, cos_wide, sin_wide, *gains_wide, gu.reshape(2, width, -1), down_weight, dall, kv,
+        qp, h1, w,
+    )
+
+    def by_columns(pieces):
+        return jnp.concatenate([pieces[i] for i in range(pieces.shape[0])], axis=1).astype(f32)
+
+    ctx = lax.axis_index("ctx")
+    heads = sums[16:18, :head_size] + sums[16:18, head_size:]
+
+    def share(row):
+        return lax.dynamic_slice_in_dim(row, ctx * (row.shape[0] // ctx_count), row.shape[0] // ctx_count)
+
     return (
         y.reshape(hidden_in.shape),
-        input_grad,
-        gains[:wide_piece],
-        total_q,
-        total_kv,
-        gains[wide_piece : wide_piece + head_piece],
-        gains[wide_piece + head_piece : wide_piece + 2 * head_piece],
-        total_out,
-        gains[wide_piece + 2 * head_piece :],
-        total_gate,
-        total_up,
-        total_down,
+        input_grad.reshape(hidden_in.shape),
+        share(sums[8:16].reshape(width)),
+        by_columns(qkvo_all[:, :, :256]),
+        by_columns(qkvo_all[:, :, 256:512]),
+        share(heads[0]),
+        share(heads[1]),
+        by_columns(qkvo_all[:, :, 512:]),
+        share(sums[0:8].reshape(width)),
+        by_columns(gate_all),
+        by_columns(up_all),
+        by_columns(down_all),
     )
 
 

time: 480 us -> 316 us (0.66)
  waiting for transfers between devices: 93.5 us -> 0 us
  Pallas kernels: 241 us -> 288 us
  local copies, waits for them, and re-layouts: 55.1 us -> 9.56 us
  other arithmetic: 35.5 us -> 11.4 us
  blocking collectives: 23.6 us -> 0 us
  between operations: 17.6 us -> 1.86 us
  matrix products: 7.62 us -> 0 us
    psum x1 -> x0, waiting for transfers between devices: 48.4 us -> none  [summed(): return lax.psum(share, 'dp').astype(f32)]
    pallas_call x1, Pallas kernels: 140 us -> 187 us  [back(): pl.pallas_call(back_kernel, out_shape=(shape((256, 1024), bf16), shape((2...]
    unnamed x6 -> x0, waiting for transfers between devices: 37.2 us -> none
    unnamed x1 -> x0, blocking collectives: 14.9 us -> none
    unnamed x54 -> x20, local copies, waits for them, and re-layouts: 16.8 us -> 2.54 us
    mul x16 -> x0, local copies, waits for them, and re-layouts: 14 us -> none  [the longest x8 9.23 us: norm_back(): value_rows * cubed]
    concatenate x2 -> x0, other arithmetic: 13.4 us -> none  [the longest x1 13.4 us: staged(): jnp.concatenate([outer_dot(h1, d_qraw), outer_dot(h1, d_kvraw), outer_dot...]
    slice x10 -> x1, local copies, waits for them, and re-layouts: 12.4 us -> 0.01 us  [staged(): heads[1]]
  transfers between devices with their start and end apart: 5 -> 0, of which waited for: 3 -> 0; matrix products, arithmetic and copies ran while one was open for 4% -> 0% of each run, Pallas kernels for 0% -> 0%
where the time goes in v2:
time: 316 us; the launch traced here: 310 us
  Pallas kernels  288 us (91%)
  other arithmetic  11.4 us (4%)
  local copies, waits for them, and re-layouts  9.56 us (3%)
    pallas_call x1, Pallas kernels, back(): pl.pallas_call(back_kernel, out_shape=(shape((256, 1024), bf16), shape((2...  187 us
    pallas_call x1, Pallas kernels, front(): pl.pallas_call(front_kernel, out_shape=(shape((256, 1024), bf16), shape((...  100 us
    convert_element_type x5, other arithmetic, by_columns(): jnp.concatenate([pieces[i] for i in range(pieces.shape[0])], axis=1)  6.93 us

profile of v2, /device:TPU:0, one launch (start us, length us, event | category | flops | bytes accessed | tf_op | source)
XLA Modules:
  0.0 310.5 jit_solution(7936794852552412424)
XLA Ops:
  0.6 0.0 copy-start.7
  0.7 0.0 copy-start.8
  0.7 0.7 dynamic-slice_multiply_fusion
  1.4 0.1 fusion.1
  1.5 0.2 fusion
  1.7 0.8 copy.27.sin_ref
  2.5 0.8 copy.26.cos_ref
  3.9 0.1 fusion.2
  4.0 1.9 bitcast_select_fusion.dffn_ref
  5.9 0.1 iota_add_fusion
  6.0 0.0 copy-start.6
  6.0 0.8 copy.28.qpos_ref
  6.8 0.7 broadcast_multiply_fusion
  7.5 0.1 add.100
  7.5 0.1 add.101
  7.6 0.6 compare_select_fusion.kpos_ref
  8.2 0.0 copy-done.7
  8.2 0.6 broadcast_in_dim_tile.6.qg_ref
  8.8 0.0 copy-done.8
  8.8 0.6 broadcast_in_dim_tile.7.kg_ref
  9.4 100.5 %front.1 = (bf16[256,1024]{1,0:T(8,128)(2,1)}, f32[256,1536]{1,0:T(8,128)}, bf16[8,512,128]{2,1,0:T(8,128)(2,1)}, bf16[8,256,1024]{2,1,0:T(8,128)(2,1)}, bf16[25...) custom-call(bf16[256,1024]{1,0:T(8,128)(2,1)} %bitcast.87, ...), custom_call_target="tpu_custom_call" | custom-call | tf_op jit(solution)/shard_map/front/pallas_call | solution.py:575
  109.9 0.0 copy-done.6
  109.9 187.2 %back.1 = (bf16[256,1024]{1,0:T(8,128)(2,1)}, f32[256,1024]{1,0:T(8,128)}, f32[24,128]{1,0:T(8,128)}, bf16[4,128,1152]{2,1,0:T(8,128)(2,1)}, bf16[4,128,1152]{2,...) custom-call(bf16[256,1024]{1,0:T(8,128)(2,1)} %bitcast.88, ...), custom_call_target="tpu_custom_call" | custom-call | tf_op jit(solution)/shard_map/back/pallas_call | solution.py:1109
  297.1 1.3 slice_bitcast_fusion.3
  298.4 0.0 copy-start
  298.5 0.0 copy-start.1
  298.5 1.7 maximum_convert_fusion.2
  300.2 0.0 copy-done
  300.2 0.7 copy-done.1
  300.9 0.2 slice_bitcast_fusion.7
  301.1 1.6 maximum_convert_fusion.1
  302.8 0.0 copy-start.3
  302.8 0.0 copy-start.5
  302.8 1.6 maximum_convert_fusion
  304.4 0.0 copy-start.4
  304.4 0.0 copy-done.3
  304.4 0.0 copy-start.2
  304.4 0.1 slice_bitcast_fusion.15
  304.5 0.8 maximum_convert_fusion.5
  305.4 0.0 copy-done.5
  305.4 0.1 slice_add_fusion
  305.4 0.6 dynamic-slice_bitcast_fusion
  306.0 1.1 maximum_convert_fusion.3
  307.1 0.6 dynamic_slice.20
  307.7 0.6 dynamic_slice.25
  308.3 0.0 copy-done.4
  308.3 0.8 copy.34
  309.1 0.0 copy-done.2
  309.1 1.0 copy.35
  (9 shorter events, 0.1 us)
Async XLA Ops:
  0.6 7.6 %copy-start.7 = (f32[64]{0:T(128)S(1)}, f32[64]{0:T(128)}, u32[]{:S(2)}) copy-start(f32[64]{0:T(128)} %param.21) | copy-start | bytes 772
  0.7 8.2 %copy-start.8 = (f32[64]{0:T(128)S(1)}, f32[64]{0:T(128)}, u32[]{:S(2)}) copy-start(f32[64]{0:T(128)} %param.22) | copy-start | bytes 772
  6.0 103.9 %copy-start.6 = (s32[2,128]{1,0:T(2,128)}, s32[2,128]{1,0:T(2,128)S(1)}, u32[]{:S(2)}) copy-start(s32[2,128]{1,0:T(2,128)S(1)} %iota_add_fusion) | copy-start | bytes 3076
  298.4 1.7 copy-start
  298.5 2.5 copy-start.1
  302.8 1.7 copy-start.3
  302.8 2.6 copy-start.5
  304.4 3.9 %copy-start.4 = (bf16[256,1024]{1,0:T(8,128)(2,1)S(1)}, bf16[256,1024]{1,0:T(8,128)(2,1)}, u32[]{:S(2)}) copy-start(bf16[256,1024]{1,0:T(8,128)(2,1)} %get-tuple-element.39) | copy-start | bytes 1572868
  304.4 4.7 %copy-start.2 = (f32[256,1024]{1,0:T(8,128)S(1)}, f32[256,1024]{1,0:T(8,128)}, u32[]{:S(2)}) copy-start(f32[256,1024]{1,0:T(8,128)} %get-tuple-element.40) | copy-start | bytes 3145732

commit v3 on v2

--- a/solution.py
+++ b/solution.py
@@ -237,367 +237,27 @@
             self.copy(*step).wait_send()
 
 
-def greet(plane, sibling, z_near, z_far):
+def greet():
     d, ctx, z, c = place_of()
     barrier = pltpu.get_barrier_semaphore()
-    count = 0
 
     def call(dp, other):
         pl.semaphore_signal(barrier, inc=1, device_id=(dp, other), device_id_type=MESH)
 
-    for k in plane:
+    for k in NEIGHBOURS:
         call(flip(d, k), ctx)
-        count += 1
-    if sibling:
-        call(d, 2 * z + 1 - c)
-        count += 1
-    if z_near == "line":
-
-        @pl.when(z > 0)
-        def _():
-            call(d, ctx - 2)
-
-        @pl.when(z < 3)
-        def _():
-            call(d, ctx + 2)
-
-        count = count + jnp.where(z > 0, 1, 0) + jnp.where(z < 3, 1, 0)
-    if z_near == "pair":
-        call(d, 2 * flip(z, 1) + c)
-        count += 1
-    if z_far:
-        call(d, 2 * flip(z, 2) + c)
-        count += 1
-    return barrier, count
-
-
-def front_kernel(
-    x_ref, norm_ref, qw_ref, kvw_ref, outw_ref, gate_ref, up_ref, dffn_ref, cos_ref, sin_ref, qg_ref,
-    kg_ref, qpos_ref, kpos_ref,
-    h1_ref, raw_ref, qp_ref, kv_ref, ob_ref, lrow_ref, w_ref, wout_ref, gu_ref, dall_ref,
-    acc_ref, sum_ref, bias_ref,
-    loc, wsend, wrecv, osend, orecv, dsend, drecv, gsend, grecv, lsend, lrecv, ssend, srecv,
-):
-    d, ctx, z, c = place_of()
-    sibling = (d, 2 * z + 1 - c)
-    slice_width = gu_ref.shape[3]
-    barrier, count = greet((1, 2, 3), True, "line", False)
-
-    def local(source, target, slot):
-        return pltpu.make_async_copy(source, target, loc.at[slot])
-
-    own = [
-        local(qw_ref, w_ref.at[d, :, pl.ds(0, 1024)], 0),
-        local(kvw_ref, w_ref.at[d, :, pl.ds(1024, 1024)], 1),
-        local(outw_ref, wout_ref.at[d], 2),
-        local(dffn_ref, dall_ref.at[0], 3),
-        local(gate_ref.at[:, pl.ds(pl.multiple_of(d * slice_width, 128), slice_width)], gu_ref.at[0, d], 4),
-        local(up_ref.at[:, pl.ds(pl.multiple_of(d * slice_width, 128), slice_width)], gu_ref.at[1, d], 5),
-    ]
-    for copy in own:
-        copy.start()
-
-    x = x_ref[...].astype(f32)
-    scale = lax.rsqrt(jnp.mean(x * x, axis=-1, keepdims=True) + epsilon)
-    h1_ref[...] = (x * scale * norm_ref[...]).astype(bf16)
-    own[0].wait()
-    own[1].wait()
-    pl.semaphore_wait(barrier, count)
-
-    half = 128
-    qkv = Gather(w_ref, wsend, wrecv, half * c, half, "absolute", True, half * (1 - c))
-    wout = Gather(wout_ref, osend, orecv, half * c, half, "absolute", True, half * (1 - c))
-    dall = Gather(dall_ref, dsend, drecv, 0, 256, "relative")
-
-    def multiply(k, first):
-        e = flip(d, k)
-        part = nn(h1_ref[:, pl.ds(pl.multiple_of(e * 256, 256), 256)], w_ref[e])
-        acc_ref[...] = part if first else acc_ref[...] + part
-
-    qkv.start()
-    multiply(0, True)
-    qkv.hop_near()
-    own[2].wait()
-    own[3].wait()
-    qkv.landed(4)
-    multiply(1, False)
-    qkv.landed(5)
-    multiply(2, False)
-    qkv.hop_far()
-
-    def spread(wait):
-        for j in NEIGHBOURS:
-            for core, weight in ((0, gate_ref), (1, up_ref)):
-
-                @pl.when(c == core)
-                def _():
-                    copy = pltpu.make_async_remote_copy(
-                        src_ref=weight.at[
-                            :, pl.ds(pl.multiple_of(flip(d, j) * slice_width, 128), slice_width)
-                        ],
-                        dst_ref=gu_ref.at[core, d],
-                        send_sem=gsend.at[j - 1],
-                        recv_sem=grecv.at[j - 1],
-                        device_id=(flip(d, j), ctx),
-                        device_id_type=MESH,
-                    )
-                    if wait:
-                        copy.wait_send()
-                    else:
-                        copy.start()
-
-    def spread_on(j):
-        return pltpu.make_async_remote_copy(
-            src_ref=gu_ref.at[c, flip(d, j)],
-            dst_ref=gu_ref.at[c, flip(d, j)],
-            send_sem=gsend.at[j + 2],
-            recv_sem=grecv.at[j + 2],
-            device_id=sibling,
-            device_id_type=MESH,
-        )
-
-    def spread_landed(slot, core, j):
-        pltpu.make_async_remote_copy(
-            src_ref=gu_ref.at[core, flip(d, j)],
-            dst_ref=gu_ref.at[core, flip(d, j)],
-            send_sem=gsend.at[slot],
-            recv_sem=grecv.at[slot],
-            device_id=sibling,
-            device_id_type=MESH,
-        ).wait_recv()
-
-    wout.start()
-    dall.start()
-    spread(False)
-    qkv.landed(6)
-    qkv.landed(7)
-    multiply(3, False)
-
-    cosine, sine = cos_ref[...], sin_ref[...]
-    low = lanes(256) < 64
-
-    def turned(u, gain):
-        normed = u * lax.rsqrt(head_sum(u * u) * (1.0 / 64) + epsilon) * gain
-        return normed * cosine + half_turn(normed) * sine
-
-    for m in range(4):
-        u = acc_ref[:, 1024 + 128 * m : 1152 + 128 * m]
-        kv_ref[ctx, :, 128 * m : 128 * (m + 1)] = turned(u, kg_ref[...]).astype(bf16)
-    kv_ref[ctx, :, 512:] = acc_ref[:, 1536:].astype(bf16)
-
-    def line_copy(slot, block, target):
-        return pltpu.make_async_remote_copy(
-            src_ref=kv_ref.at[block],
-            dst_ref=kv_ref.at[block],
-            send_sem=lsend.at[slot],
-            recv_sem=lrecv.at[slot],
-            device_id=(d, target),
-            device_id_type=MESH,
-        )
-
-    def sibling_line(slot, block):
-        return pltpu.make_async_remote_copy(
-            src_ref=kv_ref.at[block],
-            dst_ref=kv_ref.at[block],
-            send_sem=lsend.at[slot],
-            recv_sem=lrecv.at[slot],
-            device_id=sibling,
-            device_id_type=MESH,
-        )
-
-    def sibling_copy(slot, block):
-        return pltpu.make_async_remote_copy(
-            src_ref=kv_ref.at[block],
-            dst_ref=kv_ref.at[block],
-            send_sem=ssend.at[slot],
-            recv_sem=srecv.at[slot],
-            device_id=sibling,
-            device_id_type=MESH,
-        )
+    call(d, 2 * z + 1 - c)
+    call(d, 2 * flip(z, 2) + c)
+
+    @pl.when(z > 0)
+    def _():
+        call(d, ctx - 2)
 
     @pl.when(z < 3)
     def _():
-        line_copy(1, ctx, ctx + 2).start()
-
-    @pl.when(z > 0)
-    def _():
-        line_copy(2, ctx, ctx - 2).start()
-
-    sibling_copy(0, ctx).start()
-
-    for n in range(8):
-        u = turned(acc_ref[:, 128 * n : 128 * (n + 1)], qg_ref[...])
-        other = pltpu.roll(u, 64, 1)
-        if n % 2 == 0:
-            even, odd = jnp.where(low, u, 0.0), jnp.where(low, other, 0.0)
-        else:
-            even, odd = jnp.where(low, 0.0, other), jnp.where(low, 0.0, u)
-        qp_ref[n, 0:256] = even.astype(bf16)
-        qp_ref[n, 256:512] = odd.astype(bf16)
-    raw_ref[...] = acc_ref[:, 0:1536]
-
-    sum_ref[...] = jnp.zeros_like(sum_ref)
-    ones = jnp.ones((256, 128), bf16)
-    to_exponent = math.log2(math.e) / 8.0
-
-    def attend(block):
-        bias_ref[...] = jnp.where(kpos_ref[block] <= qpos_ref[...], 0.0, masked_score)
-
-        def head(n, _):
-            m = lax.div(n, 2)
-            keys = kv_ref[block, :, pl.ds(pl.multiple_of(128 * m, 128), 128)]
-            values = kv_ref[block, :, pl.ds(pl.multiple_of(512 + 128 * m, 128), 128)]
-            scores = nt(qp_ref[n], keys) * to_exponent
-            bias = bias_ref[...]
-            terms = jnp.concatenate(
-                [jnp.exp2(scores[0:256] + bias), jnp.exp2(scores[256:512] + bias)], axis=0
-            ).astype(bf16)
-            sum_ref[n] += nn(terms, jnp.concatenate([values, ones], axis=1))
-            return 0
-
-        lax.fori_loop(0, 8, head, 0)
-
-    def step(j, _):
-        k = lax.div(j + 1, 2)
-        side = lax.rem(j + 1, 2)
-        toward = jnp.where(j == 0, 0, 1 - 2 * side)
-        source = z - toward * k
-
-        @pl.when((source >= 0) & (source <= 3))
-        def _():
-            block = 2 * source + c
-            target = z + toward
-
-            @pl.when(j > 0)
-            def _():
-                sibling_line(j, block).wait_recv()
-
-                @pl.when((target >= 0) & (target <= 3))
-                def _():
-                    line_copy(j + 2, block, 2 * target + c).start()
-
-                sibling_copy(j, block).start()
-
-            attend(block)
-            mate = 2 * source + 1 - c
-            sibling_copy(j, mate).wait_recv()
-            attend(mate)
-
-        @pl.when(j == 0)
-        def _():
-            wout.hop_near()
-
-        @pl.when(j == 2)
-        def _():
-            wout.hop_far()
-            dall.hop_near()
-
-        return 0
-
-    lax.fori_loop(0, 7, step, 0)
-    for n in range(8):
-        total = sum_ref[n]
-        weight = total[:, 128:]
-        part = total[:, :128] / weight
-        even, odd = part[0:256], part[256:512]
-        if n % 2 == 0:
-            chunk = jnp.where(low, even, pltpu.roll(odd, 64, 1))
-        else:
-            chunk = jnp.where(low, pltpu.roll(even, 64, 1), odd)
-        ob_ref[:, 128 * n : 128 * (n + 1)] = chunk.astype(bf16)
-        whole = jnp.where(low, weight[0:256], weight[256:512])
-        rows = exact_nt(head_marks(n), jnp.log2(whole)) * (1.0 / 64)
-        lrow_ref[...] = rows if n == 0 else lrow_ref[...] + rows
-
-    def line_drain(j, _):
-        k = lax.div(j + 1, 2)
-        side = lax.rem(j + 1, 2)
-        toward = jnp.where(j == 0, 0, 1 - 2 * side)
-        source = z - toward * k
-
-        @pl.when((source >= 0) & (source <= 3))
-        def _():
-            block = 2 * source + c
-            target = z + toward
-            sibling_copy(j, block).wait_send()
-
-            @pl.when((j > 0) & (target >= 0) & (target <= 3))
-            def _():
-                line_copy(j + 2, block, 2 * target + c).wait_send()
-
-        return 0
-
-    lax.fori_loop(0, 7, line_drain, 0)
-
-    @pl.when(z < 3)
-    def _():
-        line_copy(1, ctx, ctx + 2).wait_send()
-
-    @pl.when(z > 0)
-    def _():
-        line_copy(2, ctx, ctx - 2).wait_send()
-
-    dall.hop_far()
-    for j in NEIGHBOURS:
-        spread_landed(j - 1, c, j)
-        spread_on(j).start()
-    for slot in (4, 5, 6, 7):
-        wout.landed(slot)
-    for j in NEIGHBOURS:
-        spread_landed(j + 2, 1 - c, j)
-        spread_on(j).wait_send()
-    spread(True)
-    qkv.drain()
-    wout.drain()
-    dall.drain()
-    own[4].wait()
-    own[5].wait()
-
-
-def vmem():
-    return pl.BlockSpec(memory_space=pltpu.VMEM)
-
-
-def anywhere():
-    return pl.BlockSpec(memory_space=pl.ANY)
-
-
-def shape(dims, dtype):
-    return jax.ShapeDtypeStruct(dims, dtype)
-
-
-def sems(n):
-    return pltpu.SemaphoreType.DMA((n,))
-
-
-def front(x, norm_in, q_weight, kv_weight, out_weight, gate_weight, up_weight, dffn, cosine, sine, q_gain, k_gain, qpos, kpos):
-    width = gate_weight.shape[1] // 4
-    return pl.pallas_call(
-        front_kernel,
-        out_shape=(
-            shape((256, 1024), bf16),
-            shape((256, 1536), f32),
-            shape((8, 512, 128), bf16),
-            shape((8, 256, 1024), bf16),
-            shape((256, 1024), bf16),
-            shape((16, 256), f32),
-            shape((4, 256, 2048), bf16),
-            shape((4, 256, 1024), bf16),
-            shape((2, 4, 256, width), bf16),
-            shape((4, 256, 1024), bf16),
-        ),
-        in_specs=[vmem(), vmem()] + [anywhere()] * 6 + [vmem()] * 6,
-        out_specs=[vmem()] * 10,
-        scratch_shapes=[
-            pltpu.VMEM((256, 2048), f32),
-            pltpu.VMEM((8, 512, 256), f32),
-            pltpu.VMEM((256, 256), f32),
-            sems(6),
-            sems(8), sems(8), sems(8), sems(8), sems(4), sems(4), sems(6), sems(6), sems(9), sems(9), sems(7), sems(7),
-        ],
-        compiler_params=pltpu.CompilerParams(collective_id=1, has_side_effects=True, vmem_limit_bytes=56 * 2**20),
-        name="front",
-    )(x, norm_in, q_weight, kv_weight, out_weight, gate_weight, up_weight, dffn, cosine, sine, q_gain, k_gain, qpos, kpos)
+        call(d, ctx + 2)
+
+    return barrier, 5 + jnp.where(z > 0, 1, 0) + jnp.where(z < 3, 1, 0)
 
 
 def remote(source, target, send, recv, device):
@@ -718,43 +378,261 @@
     copy.wait()
 
 
-def back_kernel(
-    x_ref, ob_ref, lrow_ref, nmid_ref, nin_ref, qpos_ref, kpos_ref, wout_ref, raw_ref, cos_ref, sin_ref, qg_ref, kg_ref,
-    gu_hbm, down_hbm, dall_hbm, kv_hbm, qp_hbm, h1_hbm, w_hbm,
-    y_ref, ig_ref, gains_ref, gate_all, up_all, down_all, qkvo_all,
-    gu, down, dall, kv, qp, h2, act, y1, own_p, y_out, p_out, y_in, p_in,
-    dop, dqt, bias, core_in, near_in, far_in, dcore, dsum, dnear, dfar, kcore, knear, kfar,
-    h1_all, ob_all, cols_in, wcore, wnear, wfar, piece, dpiece, gsum, gin,
-    loc, hsend, hrecv, psend, precv, ysend, yrecv, gsend, grecv, usend, urecv, dsend, drecv, asend, arecv, ksend, krecv,
-    h1send, h1recv, obsend, obrecv, csend, crecv, wsend, wrecv, agsend, agrecv, ausend, aurecv, adsend, adrecv,
-    aqsend, aqrecv, nsend, nrecv,
+def block_kernel(
+    x_ref, cot_ref, lens_ref, nin_ref, nmid_ref, cos_ref, sin_ref, qg_ref, kg_ref, qcol_ref, qrow_ref, kpos_ref,
+    qw_ref, kvw_ref, outw_ref, gate_ref, up_ref, downw_ref,
+    y_ref, ig_ref, gains_ref, gate_all, up_all, down_all, qkvo_all, w_hbm,
+    w, wout, gu, down, dall, kv, qp, ob, lrow_buf, acc, pool, bias,
+    h2, h1_all, act, y_out, p_out, part_in, dop, out_part,
+    core_in, near_in, far_in, dcore, dsum, dnear, dfar, knear, kfar,
+    cols_in, wcore, wnear, wfar, ocore, onear, ofar, ocols, gsum, gin,
+    loc, wsend, wrecv, osend, orecv, dasend, darecv, gusend, gurecv, lsend, lrecv, ssend, srecv,
+    hsend, hrecv, psend, precv, ysend, yrecv, gsend, grecv, usend, urecv, dsend, drecv, asend, arecv, ksend, krecv,
+    h1send, h1recv, csend, crecv, wssend, wsrecv, agsend, agrecv, ausend, aurecv, adsend, adrecv,
+    aqsend, aqrecv, nsend, nrecv, ossend, osrecv, ocsend, ocrecv, credit, core_credit,
 ):
     d, ctx, z, c = place_of()
     sibling = (d, 2 * z + 1 - c)
-    barrier, count = greet((1, 2, 3), True, "pair", True)
-    cut_width = act.shape[2] // 3
-    cuts = [slice(i * cut_width, (i + 1) * cut_width) for i in range(3)]
-    loads = [
-        pltpu.make_async_copy(source, target, loc.at[slot])
-        for slot, (source, target) in enumerate(
-            (
-                (gu_hbm, gu), (down_hbm, down), (dall_hbm, dall), (kv_hbm, kv), (qp_hbm, qp), (h1_hbm, h1_all.at[0]),
-            )
-        )
+    width = act.shape[2]
+    barrier, count = greet()
+
+    def local(source, target, slot):
+        copy = pltpu.make_async_copy(source, target, loc.at[slot])
+        copy.start()
+        return copy
+
+    def columns(j):
+        return pl.ds(pl.multiple_of(flip(d, j) * width, 128), width)
+
+    def block_rows(e):
+        return pl.ds(pl.multiple_of(256 * e, 256), 256)
+
+    own = [
+        local(qw_ref, w.at[d, :, pl.ds(0, 1024)], 0),
+        local(kvw_ref, w.at[d, :, pl.ds(1024, 1024)], 1),
+        local(outw_ref, wout.at[d], 2),
+        local(gate_ref.at[:, columns(0)], gu.at[0, block_rows(d)], 3),
+        local(up_ref.at[:, columns(0)], gu.at[1, block_rows(d)], 4),
+        local(downw_ref, down, 5),
+        local(cot_ref, dall.at[0], 6),
     ]
-    for copy in loads:
-        copy.start()
-    ob_all[0] = ob_ref[...]
-
-    residual = x_ref[...].astype(f32) + nn(ob_ref[...], wout_ref[...])
+    x = x_ref[...].astype(f32)
+    scale = lax.rsqrt(jnp.mean(x * x, axis=-1, keepdims=True) + epsilon)
+    h1_all[0] = (x * scale * nin_ref[...]).astype(bf16)
+    own[6].wait()
+    valid = qcol_ref[...] < lens_ref[0, 0]
+    dall[0] = jnp.where(valid, dall[0].astype(f32), 0.0).astype(bf16)
+    own[0].wait()
+    own[1].wait()
+    pl.semaphore_wait(barrier, count)
+
+    half = 128
+    qkv = Gather(w, wsend, wrecv, half * c, half, "absolute", True, half * (1 - c))
+    wout_gather = Gather(wout, osend, orecv, half * c, half, "absolute", True, half * (1 - c))
+    dall_gather = Gather(dall, dasend, darecv, 0, 256, "relative")
+    h1_gather = Gather(h1_all, h1send, h1recv, 0, 256, "relative")
+    h2_gather = Gather(h2, hsend, hrecv, 0, 256, "relative")
+
+    def multiply(k):
+        e = flip(d, k)
+        return nn(h1_all[0, :, pl.ds(pl.multiple_of(e * 256, 256), 256)], w[e])
+
+    def spread(wait):
+        for j in NEIGHBOURS:
+            for core, weight in ((0, gate_ref), (1, up_ref)):
+
+                @pl.when(c == core)
+                def _():
+                    copy = remote(
+                        weight.at[:, columns(j)],
+                        gu.at[core, block_rows(d)],
+                        gusend.at[j - 1],
+                        gurecv.at[j - 1],
+                        (flip(d, j), ctx),
+                    )
+                    if wait:
+                        copy.wait_send()
+                    else:
+                        copy.start()
+
+    def spread_on(j):
+        block = gu.at[c, block_rows(flip(d, j))]
+        return remote(block, block, gusend.at[j + 2], gurecv.at[j + 2], sibling)
+
+    def spread_landed(slot, core, j):
+        block = gu.at[core, block_rows(flip(d, j))]
+        remote(block, block, gusend.at[slot], gurecv.at[slot], sibling).wait_recv()
+
+    def spread_pass(j):
+        spread_landed(j - 1, c, j)
+        spread_on(j).start()
+
+    qkv.start()
+    acc[...] = multiply(0)
+    qkv.hop_near()
+    qkv.landed(4)
+    acc[...] += multiply(1)
+    qkv.landed(5)
+    acc[...] += multiply(2)
+    own[2].wait()
+    qkv.hop_far()
+    wout_gather.start()
+    spread(False)
+    qkv.landed(6)
+    qkv.landed(7)
+    acc[...] += multiply(3)
+
+    cosine, sine = cos_ref[...], sin_ref[...]
+    low = lanes(256) < 64
+
+    def turned(u, gain):
+        normed = u * lax.rsqrt(head_sum(u * u) * (1.0 / 64) + epsilon) * gain
+        return normed * cosine + half_turn(normed) * sine
+
+    for m in range(4):
+        u = acc[:, 1024 + 128 * m : 1152 + 128 * m]
+        kv[ctx, :, 128 * m : 128 * (m + 1)] = turned(u, kg_ref[...]).astype(bf16)
+    kv[ctx, :, 512:] = acc[:, 1536:].astype(bf16)
+
+    def line_copy(slot, block, device):
+        return remote(kv.at[block], kv.at[block], lsend.at[slot], lrecv.at[slot], device)
+
+    def sibling_copy(slot, block):
+        return remote(kv.at[block], kv.at[block], ssend.at[slot], srecv.at[slot], sibling)
+
+    @pl.when(z < 3)
+    def _():
+        line_copy(1, ctx, (d, ctx + 2)).start()
+
+    @pl.when(z > 0)
+    def _():
+        line_copy(2, ctx, (d, ctx - 2)).start()
+
+    sibling_copy(0, ctx).start()
+    keep_w = local(w, w_hbm, 13)
+
+    def padded(target, n, u):
+        other = pltpu.roll(u, 64, 1)
+        if n % 2 == 0:
+            even, odd = jnp.where(low, u, 0.0), jnp.where(low, other, 0.0)
+        else:
+            even, odd = jnp.where(low, 0.0, other), jnp.where(low, 0.0, u)
+        target[n, 0:256] = even.astype(bf16)
+        target[n, 256:512] = odd.astype(bf16)
+
+    def unpadded(n, both):
+        even, odd = both[0:256], both[256:512]
+        if n % 2 == 0:
+            return jnp.where(low, even, pltpu.roll(odd, 64, 1))
+        return jnp.where(low, pltpu.roll(even, 64, 1), odd)
+
+    for n in range(8):
+        padded(qp, n, turned(acc[:, 128 * n : 128 * (n + 1)], qg_ref[...]))
+
+    def summed(n):
+        return pool.at[512 * (n // 4) : 512 * (n // 4) + 512, 256 * (n % 4) : 256 * (n % 4) + 256]
+
+    pool[...] = jnp.zeros_like(pool)
+    ones = jnp.ones((256, 128), bf16)
+    to_exponent = math.log2(math.e) / 8.0
+
+    def attend(block):
+        bias[...] = jnp.where(kpos_ref[block] <= qcol_ref[...], 0.0, masked_score)
+        for n in range(8):
+            m = n // 2
+            keys = kv[block, :, 128 * m : 128 * (m + 1)]
+            values = kv[block, :, 512 + 128 * m : 512 + 128 * (m + 1)]
+            scores = nt(qp[n], keys) * to_exponent
+            terms = jnp.concatenate(
+                [jnp.exp2(scores[0:256] + bias[...]), jnp.exp2(scores[256:512] + bias[...])], axis=0
+            ).astype(bf16)
+            total_n = summed(n)
+            total_n[...] += nn(terms, jnp.concatenate([values, ones], axis=1))
+
+    def line_place(j):
+        k = lax.div(j + 1, 2)
+        side = lax.rem(j + 1, 2)
+        toward = jnp.where(j == 0, 0, 1 - 2 * side)
+        return z - toward * k, z + toward
+
+    def on_line(chip):
+        return (chip >= 0) & (chip <= 3)
+
+    def step(j, _):
+        source, target = line_place(j)
+
+        @pl.when(on_line(source))
+        def _():
+            block = 2 * source + c
+
+            @pl.when(j > 0)
+            def _():
+                line_copy(j, block, sibling).wait_recv()
+
+                @pl.when(on_line(target))
+                def _():
+                    line_copy(j + 2, block, (d, 2 * target + c)).start()
+
+                sibling_copy(j, block).start()
+
+            def one(i, _):
+                mate = 2 * source + 1 - c
+
+                @pl.when(i == 1)
+                def _():
+                    sibling_copy(j, mate).wait_recv()
+
+                attend(jnp.where(i == 0, block, mate))
+                return 0
+
+            lax.fori_loop(0, 2, one, 0)
+
+        @pl.when(j == 0)
+        def _():
+            wout_gather.hop_near()
+
+        @pl.when(j == 2)
+        def _():
+            wout_gather.hop_far()
+
+        @pl.when(j == 4)
+        def _():
+            dall_gather.start()
+            spread_pass(1)
+            spread_pass(2)
+
+        return 0
+
+    lax.fori_loop(0, 7, step, 0)
+    lrow = None
+    for n in range(8):
+        both = summed(n)[...]
+        weight = both[:, 128:]
+        ob[:, 128 * n : 128 * (n + 1)] = unpadded(n, both[:, :128] / weight).astype(bf16)
+        whole = jnp.where(low, weight[0:256], weight[256:512])
+        rows = exact_nt(head_marks(n), jnp.log2(whole)) * (1.0 / 64)
+        lrow = rows if lrow is None else lrow + rows
+    lrow_buf[...] = lrow
+    for slot in (4, 5, 6, 7):
+        wout_gather.landed(slot)
+
+    y1 = pool.at[0:256]
+    own_p = pool.at[256:512]
+    dqt = pool.at[512:1024]
+    residual = x_ref[...].astype(f32) + nn(ob[...], wout[...].reshape(1024, 1024))
     y1[...] = residual
     scale = lax.rsqrt(jnp.mean(residual * residual, axis=-1, keepdims=True) + epsilon)
     h2[0] = (residual * scale * nmid_ref[...]).astype(bf16)
-    pl.semaphore_wait(barrier, count)
-    gather = Gather(h2, hsend, hrecv, 0, 256, "relative")
-    gather.start()
-    for copy in loads[:3]:
-        copy.wait()
+    h2_gather.start()
+    spread_pass(3)
+    for j in NEIGHBOURS:
+        spread_landed(j + 2, 1 - c, j)
+    for i in (3, 4, 5):
+        own[i].wait()
+    keep_w.wait()
+    qkv.drain()
+    cut_width = width // 3
+    cuts = [slice(i * cut_width, (i + 1) * cut_width) for i in range(3)]
 
     def ffn(first, blocks):
         rows = 256 * blocks
@@ -766,32 +644,34 @@
             up = nn(tokens, gu[1, :, cut])
             sig = jax.nn.sigmoid(gate)
             silu = gate * sig
-            act[0, span, cut] = (silu * up).astype(bf16)
+            w[first : first + blocks, :, cut] = (silu * up).astype(bf16).reshape(blocks, 256, cut_width)
             dact = nt(cot, down[cut, :])
-            act[1, span, cut] = (dact * up * sig * (1.0 + gate * (1.0 - sig))).astype(bf16)
-            act[2, span, cut] = (dact * silu).astype(bf16)
-        part = nt(act[1, span, :], gu[0]) + nt(act[2, span, :], gu[1])
+            act[0, span, cut] = (dact * up * sig * (1.0 + gate * (1.0 - sig))).astype(bf16)
+            act[1, span, cut] = (dact * silu).astype(bf16)
+        part = nt(act[0, span, :], gu[0]) + nt(act[1, span, :], gu[1])
         if first == 0:
             own_p[...] = part
         else:
             p_out[first - 1 : first - 1 + blocks] = part.astype(bf16).reshape(blocks, 256, 1024)
 
     def ffn_out(first, blocks):
-        part = nn(act[0, first * 256 : (first + blocks) * 256, :], down[...])
+        part = nn(w[first : first + blocks, :, :width].reshape(256 * blocks, width), down[...])
         y_out[first : first + blocks] = part.astype(bf16).reshape(blocks, 256, 1024)
 
     def scatter_p(k):
-        return remote(p_out.at[k - 1], p_in.at[k - 1], psend.at[k - 1], precv.at[k - 1], (flip(d, k), ctx))
+        return remote(p_out.at[k - 1], part_in.at[k - 1], psend.at[k - 1], precv.at[k - 1], (flip(d, k), ctx))
 
     def scatter_y(k):
-        return remote(y_out.at[k], y_in.at[k - 1], ysend.at[k - 1], yrecv.at[k - 1], (flip(d, k), ctx))
+        return remote(y_out.at[k], part_in.at[k - 1], ysend.at[k - 1], yrecv.at[k - 1], (flip(d, k), ctx))
 
     ffn(0, 1)
-    gather.hop_near()
+    h2_gather.hop_near()
+    dall_gather.hop_near()
     ffn(1, 2)
     scatter_p(1).start()
     scatter_p(2).start()
-    gather.hop_far()
+    h2_gather.hop_far()
+    dall_gather.hop_far()
     ffn(3, 1)
     scatter_p(3).start()
     ffn_out(0, 1)
@@ -799,12 +679,14 @@
     ffn_out(3, 1)
 
     tokens = h2[...].reshape(1024, 1024)
-    gu[0] = tn(tokens, act[1]).astype(bf16)
+    for j in NEIGHBOURS:
+        spread_on(j).wait_send()
+    gu[0] = tn(tokens, act[0]).astype(bf16)
 
     def weight_sum(t, send, recv):
         return CtxSum(
             lambda r, core: gu.at[t, pl.ds(128 * (2 * flip(z, r) + core), 128)],
-            core_in.at[t],
+            core_in.at[:, pl.ds(128 * t, 128)],
             near_in.at[t],
             far_in.at[t],
             send,
@@ -815,17 +697,20 @@
     up_sum = weight_sum(1, usend, urecv)
     for r in (3, 1, 2, 0):
         gate_sum.begin(r)
-    gu[1] = tn(tokens, act[2]).astype(bf16)
+    gu[1] = tn(tokens, act[1]).astype(bf16)
     for r in (3, 1, 2, 0):
         up_sum.begin(r)
-    down[...] = tn(act[0], dall[...].reshape(1024, 1024)).astype(bf16)
-    half = down.shape[0] // 2
+    hidden = w[:, :, :width].reshape(1024, width)
+    down[...] = tn(hidden, dall[...].reshape(1024, 1024)).astype(bf16)
+    half_rows = down.shape[0] // 2
 
     def down_core():
-        return remote(down.at[pl.ds(half * (1 - c), half)], dcore, dsend.at[0], drecv.at[0], sibling)
+        return remote(down.at[pl.ds(half_rows * (1 - c), half_rows)], dcore, dsend.at[0], drecv.at[0], sibling)
 
     def down_piece(j):
-        return down.at[pl.ds(half * c, half), pl.ds(pl.multiple_of(256 * flip(d, j), 256), 256)]
+        return down.at[
+            pl.ds(half_rows * c, half_rows), pl.ds(pl.multiple_of(256 * flip(d, j), 256), 256)
+        ]
 
     def down_copy(j):
         return remote(down_piece(j), dsum.at[d], dsend.at[j], drecv.at[j], (flip(d, j), ctx))
@@ -844,25 +729,20 @@
 
     part_sum(gate_sum)
     part_sum(up_sum)
+    pl.semaphore_signal(core_credit, inc=1, device_id=sibling, device_id_type=MESH)
     down_core().wait_recv()
-    down_mine = down.at[pl.ds(half * c, half)]
+    down_mine = down.at[pl.ds(half_rows * c, half_rows)]
     down_mine[...] = total(down_mine, dcore).astype(bf16)
 
     dmid = own_p[...]
     for k in NEIGHBOURS:
         scatter_p(k).wait_recv()
-        dmid = dmid + p_in[k - 1].astype(f32)
+        dmid = dmid + part_in[k - 1].astype(f32)
     for k in NEIGHBOURS:
+        pl.semaphore_signal(credit, inc=1, device_id=(flip(d, k), ctx), device_id_type=MESH)
         scatter_p(k).wait_send()
-    gather.drain()
+    h2_gather.drain()
     rows_in = p_out
-
-    for j in (3, 1, 2):
-        down_copy(j).start()
-    dsum[d] = down_piece(0)[...]
-    loads[5].wait()
-    ob_gather = Gather(ob_all, obsend, obrecv, 0, 256, "relative")
-    h1_gather = Gather(h1_all, h1send, h1recv, 0, 256, "relative")
 
     residual = y1[...]
     scale = lax.rsqrt(jnp.mean(residual * residual, axis=-1, keepdims=True) + epsilon)
@@ -875,46 +755,40 @@
     )
     own_p[...] = dy
     rows_in[0] = dy.astype(bf16)
-
-    def spread(i):
-        return Spread(rows_in.at[i], cols_in.at[i], csend.at[i], crecv.at[i])
-
-    ob_gather.start()
-    spread(0).start()
-    d_mixed = nt(rows_in[0], wout_ref[...])
-    low = lanes(256) < 64
+    out_part[...] = tn(ob[...], rows_in[0]).astype(bf16).reshape(4, 256, 1024)
+    out_sum = CtxSum(
+        lambda r, core: out_part.at[flip(z, r), pl.ds(128 * core, 128)], ocore, onear, ofar, ossend, osrecv
+    )
+    for r in (3, 1, 2, 0):
+        out_sum.begin(r)
+    h1_gather.start()
+    for j in (3, 1, 2):
+        down_copy(j).start()
+    dsum[d] = down_piece(0)[...]
+
+    d_mixed = nt(rows_in[0], wout[...].reshape(1024, 1024))
     delta = None
     for n in range(8):
         u = d_mixed[:, 128 * n : 128 * (n + 1)].astype(bf16).astype(f32)
-        other = pltpu.roll(u, 64, 1)
-        if n % 2 == 0:
-            even, odd = jnp.where(low, u, 0.0), jnp.where(low, other, 0.0)
-        else:
-            even, odd = jnp.where(low, 0.0, other), jnp.where(low, 0.0, u)
-        dop[n, 0:256] = even.astype(bf16)
-        dop[n, 256:512] = odd.astype(bf16)
-        rows = exact_nt(head_marks(n), u * ob_ref[:, 128 * n : 128 * (n + 1)].astype(f32))
+        padded(dop, n, u)
+        rows = exact_nt(head_marks(n), u * ob[:, 128 * n : 128 * (n + 1)].astype(f32))
         delta = rows if delta is None else delta + rows
 
-    loads[3].wait()
-    loads[4].wait()
-    to_exponent = math.log2(math.e) / 8.0
-    dqt[...] = jnp.zeros_like(dqt)
+    dqt[...] = jnp.zeros((512, 1024), f32)
 
     def dkv_chunk(r, core):
-        block = 2 * flip(z, r) + core
-        return act.at[lax.div(block, 4), pl.ds(256 * lax.rem(block, 4), 256), pl.ds(0, 1024)]
-
-    dkv_sum = CtxSum(dkv_chunk, kcore, knear, kfar, ksend, krecv)
+        return w.at[flip(z, r), :, pl.ds(1024 * core, 1024)]
+
+    dkv_sum = CtxSum(dkv_chunk, core_in.at[:, :, pl.ds(0, 1024)], knear, kfar, ksend, krecv)
 
     def row_of(table, m):
         return jnp.concatenate([table[4 * m + i : 4 * m + i + 1, :] for i in range(4)], axis=1)
 
-    lrow = lrow_ref[...]
+    lrow = lrow_buf[...]
 
     def attend_back(block, target):
         places = jnp.broadcast_to(kpos_ref[block].astype(f32), (256, 256)).T
-        bias[...] = jnp.where(places <= qpos_ref[...].astype(f32), 0.0, masked_score)
+        bias[...] = jnp.where(places <= qrow_ref[...].astype(f32), 0.0, masked_score)
         for m in range(4):
             keys = kv[block, :, 128 * m : 128 * (m + 1)]
             values = kv[block, :, 512 + 128 * m : 512 + 128 * (m + 1)]
@@ -928,63 +802,67 @@
             dscores = (weights * (dweights - row_of(delta, m))).astype(bf16)
             target[:, 128 * m : 128 * (m + 1)] = (nn(dscores, queries) * 0.125).astype(bf16)
             target[:, 512 + 128 * m : 512 + 128 * (m + 1)] = nn(weights.astype(bf16), cot).astype(bf16)
-            dqt[m] += tn(keys, dscores)
+            dqt[128 * m : 128 * (m + 1)] += tn(keys, dscores)
 
     down_sum = CtxSum(lambda r, core: dsum.at[flip(z, r)], None, dnear, dfar, asend, arecv)
+
+    def spread_rows(i):
+        return Spread(rows_in.at[i], cols_in.at[i - 1], csend.at[i], crecv.at[i])
 
     def grad_sum(i):
         return CtxSum(
             lambda r, core: h2.at[flip(z, r), pl.ds(128 * core, 128), pl.ds(256 * i, 256)],
-            wcore.at[i],
-            wnear.at[i],
-            wfar.at[i],
-            wsend.at[i],
-            wrecv.at[i],
-        )
-
-    def grad_begin(i, tokens_all):
-        spread(i).landed()
-        grad = tn(tokens_all[...].reshape(1024, 1024), cols_in[i].reshape(1024, 256)).astype(bf16)
+            wcore.at[i - 1],
+            wnear.at[i - 1],
+            wfar.at[i - 1],
+            wssend.at[i],
+            wsrecv.at[i],
+        )
+
+    def grad_begin(i):
+        spread_rows(i).landed()
+        grad = tn(h1_all[...].reshape(1024, 1024), cols_in[i - 1].reshape(1024, 256)).astype(bf16)
         h2[:, :, 256 * i : 256 * (i + 1)] = grad.reshape(4, 256, 256)
         for r in (3, 1, 2, 0):
             grad_sum(i).begin(r)
 
+    pieces = [act.at[0, 128 * i : 128 * (i + 1)] for i in (0, 1)]
+    dpiece = act.at[1, 0:half_rows, 0:256]
+    ostage = act.at[1, half_rows : half_rows + 128, 0:1024]
     gate_gather = Gather(gate_all, agsend, agrecv, 0, 128, "absolute")
     up_gather = Gather(up_all, ausend, aurecv, 0, 128, "absolute")
-    down_gather = Gather(down_all, adsend, adrecv, 0, half, "absolute")
+    down_gather = Gather(down_all, adsend, adrecv, 0, half_rows, "absolute")
     qkvo_gather = Gather(qkvo_all, aqsend, aqrecv, 0, 128, "absolute")
 
     def publish(item, stage, target, slot, gathering):
         stage[...] = item.result().astype(bf16)
-        local_copy(stage, target.at[d], loc.at[slot])
+        local(stage, target.at[d], slot).wait()
         gathering.start()
 
     for r in (3, 1, 2, 0):
         for core in (0, 1):
             attend_back(2 * flip(z, r) + core, dkv_chunk(r, core))
+        if r == 3:
+            pl.semaphore_wait(core_credit, 1)
         dkv_sum.begin(r)
         dkv_sum.add_core(r)
         if r in (1, 3):
             dkv_sum.pass_near(r)
         if r == 3:
             gate_sum.pass_far()
-            ob_gather.hop_near()
-            h1_gather.start()
         if r == 1:
             up_sum.pass_far()
+            h1_gather.hop_near()
+            pl.semaphore_wait(credit, 3)
+            for k in NEIGHBOURS:
+                scatter_y(k).start()
+        if r == 2:
+            part_sum(out_sum)
             for j in NEIGHBOURS:
                 down_landed(j)
             down_sum.pass_near(3)
             down_sum.pass_near(1)
-            ob_gather.hop_far()
-            h1_gather.hop_near()
-            for k in NEIGHBOURS:
-                scatter_y(k).start()
-        if r == 2:
-            grad_begin(0, ob_all)
             h1_gather.hop_far()
-
-    cosine, sine = cos_ref[...], sin_ref[...]
 
     def unturn(u):
         return u * cosine - half_turn(u) * sine
@@ -995,33 +873,48 @@
         back = scale * moved - value * (scale * scale * scale) * (head_sum(moved * value) * (1.0 / 64))
         return back, jnp.sum(grad * value * scale, axis=0, keepdims=True)
 
+    dkv_sum.pass_far()
+    cosine, sine = cos_ref[...], sin_ref[...]
     qgain = None
     for n in range(8):
         m, e = n // 2, n % 2
-        turned = dqt[m, :, 512 * e : 512 * (e + 1)].T
-        even, odd = turned[0:256], turned[256:512]
-        if e == 0:
-            chunk = jnp.where(low, even, pltpu.roll(odd, 64, 1))
-        else:
-            chunk = jnp.where(low, pltpu.roll(even, 64, 1), odd)
-        back, gain = norm_unwind(unturn(chunk * 0.125), raw_ref[:, 128 * n : 128 * (n + 1)], qg_ref[...])
+        chunk = unpadded(n, dqt[128 * m : 128 * (m + 1), 512 * e : 512 * (e + 1)].T)
+        back, gain = norm_unwind(unturn(chunk * 0.125), acc[:, 128 * n : 128 * (n + 1)], qg_ref[...])
         rows_in[1, :, 128 * n : 128 * (n + 1)] = back.astype(bf16)
         qgain = gain if qgain is None else qgain + gain
     gsum[16:17, :] = qgain
-    spread(1).start()
-    weights = [
-        pltpu.make_async_copy(w_hbm.at[:, :, pl.ds(1024 * i, 1024)], kv.at[pl.ds(4 * i, 4)], loc.at[6 + 5 * i])
-        for i in (0, 1)
-    ]
-    for copy in weights:
-        copy.start()
-
-    dkv_sum.pass_far()
+    spread_rows(1).start()
+    def line_drain(j, _):
+        source, target = line_place(j)
+
+        @pl.when(on_line(source))
+        def _():
+            block = 2 * source + c
+            sibling_copy(j, block).wait_send()
+
+            @pl.when((j > 0) & on_line(target))
+            def _():
+                line_copy(j + 2, block, (d, 2 * target + c)).wait_send()
+
+        return 0
+
+    lax.fori_loop(0, 7, line_drain, 0)
+
+    @pl.when(z < 3)
+    def _():
+        line_copy(1, ctx, (d, ctx + 2)).wait_send()
+
+    @pl.when(z > 0)
+    def _():
+        line_copy(2, ctx, (d, ctx - 2)).wait_send()
+
+    weights = [local(w_hbm.at[:, :, pl.ds(1024 * i, 1024)], kv.at[pl.ds(4 * i, 4)], 7 + i) for i in (0, 1)]
+
+    publish(gate_sum, pieces[0], gate_all, 9, gate_gather)
+    grad_begin(1)
     down_sum.pass_far()
-    publish(gate_sum, piece.at[0], gate_all, 7, gate_gather)
-    grad_begin(1, h1_all)
-    part_sum(grad_sum(0))
-    publish(up_sum, piece.at[1], up_all, 8, up_gather)
+    out_sum.pass_far()
+    publish(up_sum, pieces[1], up_all, 10, up_gather)
     for copy in weights:
         copy.wait()
     dh1 = nt(rows_in[1], kv[0:4].reshape(1024, 1024))
@@ -1029,20 +922,21 @@
     out = y1[...] + y_out[0].astype(f32)
     for k in NEIGHBOURS:
         scatter_y(k).wait_recv()
-        out = out + y_in[k - 1].astype(f32)
-    y_ref[...] = out.astype(bf16)
+        out = out + part_in[k - 1].astype(f32)
+    y_out[0] = out.astype(bf16)
+    y_save = local(y_out.at[0], y_ref, 14)
     part_sum(grad_sum(1))
 
     dkv = dkv_sum.result()
     kgain = None
     for n in range(4):
         span = slice(128 * n, 128 * (n + 1))
-        back, gain = norm_unwind(unturn(dkv[:, span]), raw_ref[:, 1024 + 128 * n : 1152 + 128 * n], kg_ref[...])
+        back, gain = norm_unwind(unturn(dkv[:, span]), acc[:, 1024 + 128 * n : 1152 + 128 * n], kg_ref[...])
         rows_in[2, :, span] = back.astype(bf16)
         kgain = gain if kgain is None else kgain + gain
     rows_in[2, :, 512:] = dkv[:, 512:].astype(bf16)
     gsum[17:18, :] = kgain
-    spread(2).start()
+    spread_rows(2).start()
     dh1 = dh1 + nt(rows_in[2], kv[4:8].reshape(1024, 1024))
     x = x_ref[...].astype(f32)
     scale = lax.rsqrt(jnp.mean(x * x, axis=-1, keepdims=True) + epsilon)
@@ -1056,33 +950,38 @@
 
     gain_copy(0, sibling).start()
     scaled = dh1 * nin_ref[...]
-    ig_ref[...] = own_p[...] + scale * scaled - x * (scale * scale * scale) * jnp.mean(
+    own_p[...] = own_p[...] + scale * scaled - x * (scale * scale * scale) * jnp.mean(
         scaled * x, axis=-1, keepdims=True
     )
-    grad_begin(2, h1_all)
+    ig_save = local(own_p, ig_ref, 15)
+    grad_begin(2)
     gain_copy(0, sibling).wait()
     gsum[...] = gsum[...] + gin[0]
     for k in NEIGHBOURS:
         gain_copy(k, (flip(d, k), ctx)).start()
     part_sum(grad_sum(2))
-    grad_sum(0).pass_far()
     grad_sum(1).pass_far()
+    ostage[...] = out_sum.result().astype(bf16)
+    out_spread = Spread(ostage, ocols, ocsend, ocrecv)
+    out_spread.start()
     up_gather.hop_near()
     gate_gather.hop_far()
-    publish(down_sum, dpiece, down_all, 9, down_gather)
+    publish(down_sum, dpiece, down_all, 11, down_gather)
     for k in NEIGHBOURS:
         gain_copy(k, (flip(d, k), ctx)).wait()
     gsum[...] = gsum[...] + gin[1] + gin[2] + gin[3]
     gain_copy(4, (d, 2 * flip(z, 1) + c)).start()
     grad_sum(2).pass_far()
     up_gather.hop_far()
+    out_spread.landed()
+    pieces[0][:, 512:768] = total(ocols.at[0], ocols.at[1], ocols.at[2], ocols.at[3]).astype(bf16)
     gain_copy(4, (d, 2 * flip(z, 1) + c)).wait()
     gsum[...] = gsum[...] + gin[4]
     gain_copy(5, (d, 2 * flip(z, 2) + c)).start()
     down_gather.hop_near()
-    for i, at in ((0, 512), (1, 0), (2, 256)):
-        piece[0, :, at : at + 256] = grad_sum(i).result().astype(bf16)
-    local_copy(piece.at[0, :, pl.ds(0, 768)], qkvo_all.at[d], loc.at[10])
+    for i in (1, 2):
+        pieces[0][:, 256 * (i - 1) : 256 * i] = grad_sum(i).result().astype(bf16)
+    local(pieces[0].at[:, pl.ds(0, 768)], qkvo_all.at[d], 12).wait()
     qkvo_gather.start()
     gain_copy(5, (d, 2 * flip(z, 2) + c)).wait()
     gains_ref[...] = gsum[...] + gin[5]
@@ -1090,24 +989,46 @@
     qkvo_gather.hop_near()
     qkvo_gather.hop_far()
 
-    for gathering in (ob_gather, h1_gather, gate_gather, up_gather, down_gather, qkvo_gather):
+    y_save.wait()
+    ig_save.wait()
+    for gathering in (wout_gather, dall_gather, h1_gather, gate_gather, up_gather, down_gather, qkvo_gather):
         gathering.drain()
+    spread(True)
     for k in NEIGHBOURS:
         scatter_y(k).wait_send()
         down_copy(k).wait_send()
     down_core().wait_send()
-    for item in (gate_sum, up_sum, dkv_sum, grad_sum(0), grad_sum(1), grad_sum(2)):
+    for item in (gate_sum, up_sum, dkv_sum, out_sum, grad_sum(1), grad_sum(2)):
         item.drain()
     down_sum.drain(core=False)
-    for i in range(3):
-        spread(i).drain()
-
-
-def back(x, ob, lrow, norm_mid, norm_in, qpos, kpos, wout, raw, cosine, sine, q_gain, k_gain, gu, down, dall, kv, qp, h1, w):
-    width = gu.shape[2]
+    for item in (spread_rows(1), spread_rows(2), out_spread):
+        item.drain()
+
+
+def vmem():
+    return pl.BlockSpec(memory_space=pltpu.VMEM)
+
+
+def anywhere():
+    return pl.BlockSpec(memory_space=pl.ANY)
+
+
+def shape(dims, dtype):
+    return jax.ShapeDtypeStruct(dims, dtype)
+
+
+def sems(*dims):
+    return pltpu.SemaphoreType.DMA(dims)
+
+
+def block(*operands):
+    width = operands[15].shape[1] // 4
     half = width // 2
+    b16, b32 = [
+        (lambda dtype: lambda *dims: pltpu.VMEM(dims, dtype))(dtype) for dtype in (bf16, f32)
+    ]
     return pl.pallas_call(
-        back_kernel,
+        block_kernel,
         out_shape=(
             shape((256, 1024), bf16),
             shape((256, 1024), f32),
@@ -1116,55 +1037,61 @@
             shape((4, 128, width), bf16),
             shape((4, half, 256), bf16),
             shape((4, 128, 768), bf16),
+            shape((4, 256, 2048), bf16),
         ),
-        in_specs=[vmem()] * 13 + [anywhere()] * 7,
-        out_specs=[vmem()] * 3 + [anywhere()] * 4,
+        in_specs=[vmem(), anywhere(), pl.BlockSpec(memory_space=pltpu.SMEM)] + [vmem()] * 9 + [anywhere()] * 6,
+        out_specs=[anywhere()] * 2 + [vmem()] + [anywhere()] * 5,
         scratch_shapes=[
-            pltpu.VMEM((2, 1024, width), bf16),
-            pltpu.VMEM((width, 1024), bf16),
-            pltpu.VMEM((4, 256, 1024), bf16),
-            pltpu.VMEM((8, 256, 1024), bf16),
-            pltpu.VMEM((8, 512, 128), bf16),
-            pltpu.VMEM((4, 256, 1024), bf16),
-            pltpu.VMEM((3, 1024, width), bf16),
-            pltpu.VMEM((256, 1024), f32),
-            pltpu.VMEM((256, 1024), f32),
-            pltpu.VMEM((4, 256, 1024), bf16),
-            pltpu.VMEM((3, 256, 1024), bf16),
-            pltpu.VMEM((3, 256, 1024), bf16),
-            pltpu.VMEM((3, 256, 1024), bf16),
-            pltpu.VMEM((8, 512, 128), bf16),
-            pltpu.VMEM((4, 128, 1024), f32),
-            pltpu.VMEM((256, 256), f32),
-            pltpu.VMEM((2, 4, 128, width), bf16),
-            pltpu.VMEM((2, 2, 128, width), bf16),
-            pltpu.VMEM((2, 128, width), bf16),
-            pltpu.VMEM((half, 1024), bf16),
-            pltpu.VMEM((4, half, 256), bf16),
-            pltpu.VMEM((2, half, 256), bf16),
-            pltpu.VMEM((half, 256), bf16),
-            pltpu.VMEM((4, 256, 1024), bf16),
-            pltpu.VMEM((2, 256, 1024), bf16),
-            pltpu.VMEM((256, 1024), bf16),
-            pltpu.VMEM((4, 256, 1024), bf16),
-            pltpu.VMEM((4, 256, 1024), bf16),
-            pltpu.VMEM((3, 4, 256, 256), bf16),
-            pltpu.VMEM((3, 4, 128, 256), bf16),
-            pltpu.VMEM((3, 2, 128, 256), bf16),
-            pltpu.VMEM((3, 128, 256), bf16),
-            pltpu.VMEM((2, 128, width), bf16),
-            pltpu.VMEM((half, 256), bf16),
-            pltpu.VMEM((24, 128), f32),
-            pltpu.VMEM((6, 24, 128), f32),
-            sems(12), sems(4), sems(4), sems(3), sems(3), sems(3), sems(3), sems(7), sems(7), sems(7), sems(7),
-            sems(4), sems(4), sems(7), sems(7), sems(7), sems(7), sems(4), sems(4), sems(4), sems(4),
-            pltpu.SemaphoreType.DMA((3, 4)), pltpu.SemaphoreType.DMA((3, 4)),
-            pltpu.SemaphoreType.DMA((3, 7)), pltpu.SemaphoreType.DMA((3, 7)),
+            b16(4, 256, 2048),
+            b16(4, 256, 1024),
+            b16(2, 1024, width),
+            b16(width, 1024),
+            b16(4, 256, 1024),
+            b16(8, 256, 1024),
+            b16(8, 512, 128),
+            b16(256, 1024),
+            b32(16, 256),
+            b32(256, 2048),
+            b32(1024, 1024),
+            b32(256, 256),
+            b16(4, 256, 1024),
+            b16(4, 256, 1024),
+            b16(2, 1024, width),
+            b16(4, 256, 1024),
+            b16(3, 256, 1024),
+            b16(3, 256, 1024),
+            b16(8, 512, 128),
+            b16(4, 256, 1024),
+            b16(4, 256, width),
+            b16(2, 2, 128, width),
+            b16(2, 128, width),
+            b16(half, 1024),
+            b16(4, half, 256),
+            b16(2, half, 256),
+            b16(half, 256),
+            b16(2, 256, 1024),
+            b16(256, 1024),
+            b16(2, 4, 256, 256),
+            b16(2, 4, 128, 256),
+            b16(2, 2, 128, 256),
+            b16(2, 128, 256),
+            b16(4, 128, 1024),
+            b16(2, 128, 1024),
+            b16(128, 1024),
+            b16(4, 128, 256),
+            b32(24, 128),
+            b32(6, 24, 128),
+            sems(16),
+            sems(8), sems(8), sems(8), sems(8), sems(4), sems(4), sems(6), sems(6), sems(9), sems(9), sems(7), sems(7),
+            sems(4), sems(4), sems(3), sems(3), sems(3), sems(3), sems(7), sems(7), sems(7), sems(7),
+            sems(4), sems(4), sems(7), sems(7), sems(7), sems(7), sems(4), sems(4),
+            sems(3, 4), sems(3, 4), sems(3, 7), sems(3, 7),
             sems(4), sems(4), sems(4), sems(4), sems(4), sems(4), sems(4), sems(4), sems(6), sems(6),
+            sems(7), sems(7), sems(4), sems(4), pltpu.SemaphoreType.REGULAR, pltpu.SemaphoreType.REGULAR,
         ],
-        compiler_params=pltpu.CompilerParams(collective_id=2, has_side_effects=True, vmem_limit_bytes=63 * 2**20),
-        name="back",
-    )(x, ob, lrow, norm_mid, norm_in, qpos, kpos, wout, raw, cosine, sine, q_gain, k_gain, gu, down, dall, kv, qp, h1, w)
+        compiler_params=pltpu.CompilerParams(collective_id=1, has_side_effects=True, vmem_limit_bytes=63 * 2**20),
+        name="block",
+    )(*operands)
 
 
 def staged(
@@ -1185,17 +1112,10 @@
     cos_wide = jnp.tile(cosine[:, 0, :], (1, 4))
     sin_wide = jnp.tile(jnp.concatenate([-sine_table[:, 0, :], sine_table[:, 0, :]], axis=1), (1, 2))
     x = hidden_in.reshape(tokens, width)
-    valid = (query_pos < lengths[0])[:, None]
-    dffn = jnp.where(valid, cotangent.reshape(tokens, width), jnp.zeros((), bf16))
-    gains_wide = (jnp.tile(q_gain, 2)[None], jnp.tile(k_gain, 2)[None])
-    h1, raw, qp, kv, ob, lrow, w, wout, gu, dall = front(
-        x, norm_in[None], q_weight, kv_weight, out_weight, gate_weight, up_weight, dffn, cos_wide, sin_wide,
-        *gains_wide, query_pos[:, None], key_pos.reshape(ctx_count, 1, -1),
-    )
-    y, input_grad, sums, gate_all, up_all, down_all, qkvo_all = back(
-        x, ob, lrow, norm_mid[None], norm_in[None], query_pos[None], key_pos.reshape(ctx_count, 1, -1),
-        wout.reshape(width, width), raw, cos_wide, sin_wide, *gains_wide, gu.reshape(2, width, -1), down_weight, dall, kv,
-        qp, h1, w,
+    y, input_grad, sums, gate_all, up_all, down_all, qkvo_all, _ = block(
+        x, cotangent.reshape(tokens, width), lengths.reshape(1, 1), norm_in[None], norm_mid[None], cos_wide, sin_wide,
+        jnp.tile(q_gain, 2)[None], jnp.tile(k_gain, 2)[None], query_pos[:, None], query_pos[None],
+        key_pos.reshape(ctx_count, 1, -1), q_weight, kv_weight, out_weight, gate_weight, up_weight, down_weight,
     )
 
     def by_columns(pieces):

time: 316 us -> 292 us (0.924)
  Pallas kernels: 288 us -> 266 us
    pallas_call x2 -> x1, Pallas kernels: 288 us -> 266 us  [block(): pl.pallas_call(block_kernel, out_shape=(shape((256, 1024), bf16), shape((...]
where the time goes in v3:
time: 292 us; the launch traced here: 287 us
  Pallas kernels  266 us (91%)
  local copies, waits for them, and re-layouts  10.9 us (4%)
  other arithmetic  9.38 us (3%)
    pallas_call x1, Pallas kernels, block(): pl.pallas_call(block_kernel, out_shape=(shape((256, 1024), bf16), shape((...  266 us
    convert_element_type x5, other arithmetic, by_columns(): jnp.concatenate([pieces[i] for i in range(pieces.shape[0])], axis=1)  6.93 us

profile of v3, /device:TPU:0, one launch (start us, length us, event | category | flops | bytes accessed | tf_op | source)
XLA Modules:
  0.0 287.5 jit_solution(7277980027569588218)
XLA Ops:
  0.6 0.7 dynamic-slice_multiply_fusion
  1.4 0.1 fusion.1
  1.5 0.2 fusion
  1.7 0.8 copy.27.sin_ref
  2.5 0.8 copy.26.cos_ref
  3.2 0.1 iota_add_fusion
  3.3 0.0 copy-start.6
  3.3 0.8 copy.28.qcol_ref
  4.8 0.7 broadcast_multiply_fusion
  5.4 0.1 add.98
  5.5 0.1 add.99
  5.6 0.6 compare_select_fusion.kpos_ref
  6.2 0.7 tile.16
  6.9 0.6 broadcast_in_dim_tile.6.qg_ref
  7.4 0.7 tile.34
  8.1 0.6 broadcast_in_dim_tile.7.kg_ref
  8.7 0.0 copy-done.6
  8.7 265.6 %block.1 = (bf16[256,1024]{1,0:T(8,128)(2,1)}, f32[256,1024]{1,0:T(8,128)}, f32[24,128]{1,0:T(8,128)}, bf16[4,128,1152]{2,1,0:T(8,128)(2,1)}, bf16[4,128,1152]{2...) custom-call(bf16[256,1024]{1,0:T(8,128)(2,1)} %bitcast.80, ...), custom_call_target="tpu_custom_call" | custom-call | tf_op jit(solution)/shard_map/block/pallas_call | solution.py:1030
  274.3 1.3 slice_bitcast_fusion.3
  275.7 0.0 copy-start
  275.7 0.0 copy-start.1
  275.7 1.7 maximum_convert_fusion.2
  277.4 0.0 copy-done
  277.4 0.7 copy-done.1
  278.1 0.2 slice_bitcast_fusion.7
  278.3 1.6 maximum_convert_fusion.1
  280.0 0.0 copy-start.3
  280.0 0.0 copy-start.5
  280.0 1.6 maximum_convert_fusion
  281.6 0.0 copy-start.4
  281.6 0.0 copy-done.3
  281.6 0.0 copy-start.2
  281.6 0.1 slice_bitcast_fusion.15
  281.7 0.8 maximum_convert_fusion.5
  282.6 0.0 copy-done.5
  282.6 0.1 slice_add_fusion
  282.6 0.6 dynamic-slice_bitcast_fusion
  283.2 1.1 maximum_convert_fusion.3
  284.3 0.6 dynamic_slice.20
  284.9 0.6 dynamic_slice.25
  285.5 0.0 copy-done.4
  285.5 0.8 copy.32
  286.3 0.0 copy-done.2
  286.3 1.0 copy.33
  (7 shorter events, 0.0 us)
Async XLA Ops:
  3.3 5.4 %copy-start.6 = (s32[2,128]{1,0:T(2,128)}, s32[2,128]{1,0:T(2,128)S(1)}, u32[]{:S(2)}) copy-start(s32[2,128]{1,0:T(2,128)S(1)} %iota_add_fusion) | copy-start | bytes 3076
  275.7 1.7 copy-start
  275.7 2.5 copy-start.1
  280.0 1.7 copy-start.3
  280.0 2.6 copy-start.5
  281.6 3.9 %copy-start.4 = (bf16[256,1024]{1,0:T(8,128)(2,1)S(1)}, bf16[256,1024]{1,0:T(8,128)(2,1)}, u32[]{:S(2)}) copy-start(bf16[256,1024]{1,0:T(8,128)(2,1)} %get-tuple-element.19) | copy-start | bytes 1572868
  281.6 4.7 %copy-start.2 = (f32[256,1024]{1,0:T(8,128)S(1)}, f32[256,1024]{1,0:T(8,128)}, u32[]{:S(2)}) copy-start(f32[256,1024]{1,0:T(8,128)} %get-tuple-element.20) | copy-start | bytes 3145732
